TPU v7x, 256 devices: a whole 4x4x8 slice. The times are simulated.
256 devices in a mesh: geo: 64 (over z, y, core), spec: 4 (over x).
Axes of the slice: x: 4, y: 4, z: 8, core: 2. Of those that a mesh axis runs over, the one named last changes fastest.
Arguments:
- spectrum: float32 [50, 36, 128, 512], P(None, None, 'geo', 'spec'), may hold values from 0.05 to 1
- wind_speed: float32 [128, 512], P('geo', 'spec'), may hold values from 5 to 20
- wind_dir: float32 [128, 512], P('geo', 'spec'), may hold values from -3.140625 to 3.140625
- current_u: float32 [128, 512], P('geo'), may hold values from -1 to 1
- current_v: float32 [128, 512], P('geo'), may hold values from -1 to 1
- refract_x: float32 [128, 512], P('geo'), may hold values from -1e-05 to 1e-05
- refract_y: float32 [128, 512], P('geo'), may hold values from -1e-05 to 1e-05
- land_mask: int32 [128, 512], P('geo'), may hold values 0 or 1
Outputs:
- new_spectrum: float32 [50, 36, 128, 512], P(None, None, 'geo', 'spec')
All inputs are finite; a program needn't handle non-finite values. No bound on the sum of `land_mask` on one device may be relied on, other than what follows from the above.
Results may differ from a plain program's by a relative error of at most 0.00015.
Values sent between devices are 32-bit elements; how exact they have to be, the bound alone decides.
No kernel may reach another device: no remote copies, remote signals or barrier semaphores. Data moves between devices by JAX's collectives and lax.ppermute only.
A program may use at most 128 MiB of HBM per device.

v0:
```python
import functools
import math

import jax
import jax.numpy as jnp
from jax import lax
from jax.experimental import pallas as pl
from jax.experimental.pallas import tpu as pltpu
from jax.sharding import PartitionSpec as P

gravity = 9.81
lowest_radian = 2.0 * math.pi * 0.0373
log_span = 49.0 * math.log(1.1)
wind_coef = 1.7e-06
break_coef = 2.5e-05
steep_ref = 480.0
wind_factor = 1.1
source_seconds = 360.0
courant_cells = 0.02
substep_seconds = 180.0

NF = 50
ND = 36
LANES = 128
SUB = 8
GROUPS = 7
PADF = SUB * GROUPS
RATIO = log_span / (NF - 1)
DTH = 2.0 * math.pi / ND
COS = [math.cos(DTH * i) for i in range(ND)]
SIN = [math.sin(DTH * i) for i in range(ND)]
GSPEED = [gravity / (2.0 * lowest_radian * math.exp(RATIO * j)) for j in range(NF)]
FIRST = [
    min(j for j in range(NF) if GSPEED[j] * SIN[i] > -1.001) // SUB for i in range(ND)
]
RANK = [0] * ND
for place, i_of in enumerate(sorted(range(ND), key=lambda i: (FIRST[i], i))):
    RANK[i_of] = place
COUNT = [sum(1 for i in range(ND) if FIRST[i] <= g) for g in range(GROUPS)]
BASE = [SUB * sum(COUNT[:g]) for g in range(GROUPS)]
SPARE = SUB * sum(COUNT)
PACKET = SPARE + SUB
FIELD = 2 * ND * PADF
SIDE = 2 * PADF
F32 = jnp.float32


def mirrored(i):
    return (ND - i) % ND


def group_base(group):
    total = 0
    for g in range(GROUPS - 1):
        total = total + jnp.where(group > g, SUB * COUNT[g], 0)
    return total


def slot(base, group, i):
    place = base + SUB * RANK[i]
    if FIRST[i] > 0:
        place = jnp.where(group >= FIRST[i], place, SPARE)
    return pl.ds(pl.multiple_of(place, SUB), SUB)


def field_rows(group, r, i):
    return pl.ds(pl.multiple_of((r * ND + i) * PADF + group * SUB, SUB), SUB)


def side_rows(group, r):
    return pl.ds(pl.multiple_of(r * PADF + group * SUB, SUB), SUB)


def radian_of(group):
    j = lax.broadcasted_iota(jnp.int32, (SUB, LANES), 0) + group * SUB
    return lowest_radian * jnp.exp(j.astype(F32) * RATIO), j


def position():
    odd = lax.rem(lax.axis_index("geo"), 2)
    col = pl.multiple_of(lax.axis_index("spec") * LANES, LANES)
    sign = jnp.where(odd == 1, -1.0, 1.0).astype(F32)
    return odd, col, sign


def row_of(ref, odd, r, col):
    window = (ref[...] if col is None else ref[:, pl.ds(col, LANES)]).astype(F32)
    first, second = window[0:1], window[1:2]
    own, other = (first, second) if r == 0 else (second, first)
    return jnp.where(odd == 1, other, own)


def spread(row):
    return jnp.broadcast_to(row, (SUB, LANES))


def lane_ids():
    return lax.broadcasted_iota(jnp.int32, (SUB, LANES), 1)


def emit(group, base, i, energy, cx, cy, lane, pair, gather, cross_ref, chip_ref):
    cross_ref[slot(base, group, mirrored(i)), :] = jnp.maximum(-cy[0], 0.0) * energy[0]
    chip_ref[slot(base, group, i), :] = jnp.maximum(cy[1], 0.0) * energy[1]
    out = []
    for r in range(2):
        speed = jnp.where(lane == 0, jnp.minimum(cx[r], 0.0), jnp.maximum(cx[r], 0.0))
        moved = pltpu.roll(speed * energy[r], 2 * i + 2, 1)
        out.append(jnp.where(pair == i + 1, moved, gather[r]))
    return out


def finish_packets(cross_ref, chip_ref):
    blank = jnp.zeros((SUB, LANES), F32)
    cross_ref[SPARE:PACKET, :] = blank
    chip_ref[SPARE:PACKET, :] = blank


def source_kernel(
    spec_hbm, ws_ref, wd_ref, u_ref, v_ref, sea_ref, e_ref, cross_ref, chip_ref, side_ref, raw, sem
):
    odd, col, sign = position()
    copy = pltpu.make_async_copy(spec_hbm, raw.at[pl.ds(0, NF * 2 * ND)], sem)
    copy.start()
    raw[NF * 2 * ND :, :] = jnp.zeros(((PADF - NF) * 2 * ND, LANES), F32)
    copy.wait()

    def stats(group, sums):
        s, j = radian_of(group)
        valid = j < NF
        w1 = jnp.where(valid, s * ((math.exp(RATIO) - 1.0) * DTH), 0.0)
        w2 = jnp.where(valid, (math.exp(RATIO) - 1.0) * DTH, 0.0)
        out = []
        for r in range(2):
            parts = [None, None, None, None]
            r_from = jnp.where(odd == 1, 1 - r, r)
            for i in range(ND):
                i_from = jnp.where(odd == 1, 2 * mirrored(i), 2 * i)
                got = raw[pl.ds(group * (SUB * 2 * ND) + i_from + r_from, SUB, stride=2 * ND), :]
                e_ref[field_rows(group, r, i), :] = got
                k = i % 4
                parts[k] = got if parts[k] is None else parts[k] + got
            part = (parts[0] + parts[1]) + (parts[2] + parts[3])
            out.append((sums[r][0] + part * w1, sums[r][1] + part * w2))
        return tuple(out)

    blank = jnp.zeros((SUB, LANES), F32)
    sums = lax.fori_loop(0, GROUPS, stats, ((blank, blank), (blank, blank)))
    wind_x, wind_y, sea, decay, u, v = [], [], [], [], [], []
    for r in range(2):
        total = jnp.sum(sums[r][0], axis=0, keepdims=True)
        inverse = jnp.sum(sums[r][1], axis=0, keepdims=True)
        mean_sigma = total / inverse
        mean_k = mean_sigma * mean_sigma / gravity
        ratio = total * mean_k * mean_k / steep_ref
        decay.append(spread(source_seconds * break_coef * ratio * ratio / mean_sigma))
        strength = row_of(ws_ref, odd, r, None) * (wind_factor / gravity)
        angle = row_of(wd_ref, odd, r, None) * sign
        wind_x.append(spread(strength * jnp.cos(angle)))
        wind_y.append(spread(strength * jnp.sin(angle)))
        sea.append(spread(row_of(sea_ref, odd, r, col)))
        u.append(spread(courant_cells * row_of(u_ref, odd, r, col)))
        v.append(spread(courant_cells * sign * row_of(v_ref, odd, r, col)))
    lane = lane_ids()
    pair = lax.shift_right_logical(lane + 1, 1)

    def source(group, carry):
        s, _ = radian_of(group)
        fc = (courant_cells * gravity / 2.0) / s
        gain = s * (source_seconds * wind_coef)
        damp = [sea[r] / (1.0 + decay[r] * s * s) for r in range(2)]
        base = group_base(group)
        gather = [blank, blank]
        for i in range(ND):
            energy, cx, cy = [], [], []
            for r in range(2):
                rows = field_rows(group, r, i)
                align = wind_x[r] * COS[i] + wind_y[r] * SIN[i]
                growth = gain * jnp.maximum(s * align - 1.0, 0.0)
                new = e_ref[rows, :] * damp[r] * (1.0 + growth)
                e_ref[rows, :] = new
                energy.append(new)
                cx.append(fc * COS[i] + u[r])
                cy.append(fc * SIN[i] + v[r])
            gather = emit(
                group, base, i, energy, cx, cy, lane, pair, gather, cross_ref, chip_ref
            )
        for r in range(2):
            side_ref[side_rows(group, r), :] = gather[r]
        return carry

    lax.fori_loop(0, GROUPS, source, 0)
    finish_packets(cross_ref, chip_ref)


def transport_kernel(
    last, e_ref, cross_in, chip_in, west_in, east_in, u_ref, v_ref, rx_ref, ry_ref, sea_ref, *rest
):
    if last:
        out_hbm, work, turn, sem = rest
    else:
        out_ref, cross_ref, chip_ref, side_ref, turn = rest
    odd, col, sign = position()
    sea, u, v = [], [], []
    for r in range(2):
        sea.append(spread(row_of(sea_ref, odd, r, col)))
        u.append(spread(courant_cells * row_of(u_ref, odd, r, col)))
        v.append(spread(courant_cells * sign * row_of(v_ref, odd, r, col)))
        rx = row_of(rx_ref, odd, r, col)
        ry = sign * row_of(ry_ref, odd, r, col)
        for i in range(ND):
            turn[r * ND + i : r * ND + i + 1, :] = SIN[i] * rx - COS[i] * ry
    lane = lane_ids()
    pair = lax.shift_right_logical(lane + 1, 1)
    odd_lane = lax.rem(lane, 2) == 1
    blank = jnp.zeros((SUB, LANES), F32)

    def substep(group, carry):
        s, _ = radian_of(group)
        c = (gravity / 2.0) / s
        fc = courant_cells * c
        tc = (substep_seconds / DTH) * c
        base = group_base(group)
        border = []
        for r in range(2):
            rows = side_rows(group, r)
            border.append(
                jnp.where(odd_lane, west_in[rows, :], pltpu.roll(east_in[rows, :], LANES - 2, 1))
            )

        def turned(r, i):
            energy = e_ref[field_rows(group, r, i), :]
            speed = tc * spread(turn[r * ND + i : r * ND + i + 1, :])
            return energy, jnp.maximum(speed, 0.0) * energy, jnp.minimum(speed, 0.0) * energy

        before = [turned(r, ND - 1)[1] for r in range(2)]
        first = [turned(r, 0) for r in range(2)]
        here = first
        gather = [blank, blank]
        for i in range(ND):
            after = [turned(r, i + 1) for r in range(2)] if i + 1 < ND else first
            cx = [fc * COS[i] + u[r] for r in range(2)]
            cy = [fc * SIN[i] + v[r] for r in range(2)]
            energy = [here[r][0] for r in range(2)]
            py = [jnp.maximum(cy[r], 0.0) * energy[r] for r in range(2)]
            my = [jnp.minimum(cy[r], 0.0) * energy[r] for r in range(2)]
            from_cross = cross_in[slot(base, group, i), :]
            from_chip = chip_in[slot(base, group, mirrored(i)), :]
            in_y = [from_cross - my[1], py[0] + from_chip]
            new = []
            for r in range(2):
                px = jnp.maximum(cx[r], 0.0) * energy[r]
                mx = jnp.minimum(cx[r], 0.0) * energy[r]
                brought = pltpu.roll(border[r], (LANES - (2 * i + 1)) % LANES, 1)
                px_in = jnp.where(lane == 0, brought, pltpu.roll(px, 1, 1))
                mx_in = jnp.where(lane == LANES - 1, brought, pltpu.roll(mx, LANES - 1, 1))
                stay = energy[r] - (px - mx) - (py[r] - my[r]) - (here[r][1] - here[r][2])
                gained = (px_in - mx_in) + in_y[r] + (before[r] - after[r][2])
                new.append(sea[r] * (stay + gained))
            if last:
                for r in range(2):
                    i_to = jnp.where(odd == 1, 2 * mirrored(i), 2 * i)
                    r_to = jnp.where(odd == 1, 1 - r, r)
                    work[pl.ds(group * (SUB * 2 * ND) + i_to + r_to, SUB, stride=2 * ND), :] = new[r]
            else:
                for r in range(2):
                    out_ref[field_rows(group, r, i), :] = new[r]
                gather = emit(
                    group, base, i, new, cx, cy, lane, pair, gather, cross_ref, chip_ref
                )
            before = [here[r][1] for r in range(2)]
            here = after
        if not last:
            for r in range(2):
                side_ref[side_rows(group, r), :] = gather[r]
        return carry

    lax.fori_loop(0, GROUPS, substep, 0)
    if last:
        copy = pltpu.make_async_copy(work.at[pl.ds(0, NF * 2 * ND)], out_hbm, sem)
        copy.start()
        copy.wait()
    else:
        finish_packets(cross_ref, chip_ref)


VMEM = pl.BlockSpec(memory_space=pltpu.VMEM)
ANY = pl.BlockSpec(memory_space=pl.ANY)
PARAMS = pltpu.CompilerParams(vmem_limit_bytes=24 * 1024 * 1024)


def packets():
    return [
        jax.ShapeDtypeStruct((FIELD, LANES), F32),
        jax.ShapeDtypeStruct((PACKET, LANES), F32),
        jax.ShapeDtypeStruct((PACKET, LANES), F32),
        jax.ShapeDtypeStruct((SIDE, LANES), F32),
    ]


def exchange(cross, chip, side):
    geo, spec = lax.axis_size("geo"), lax.axis_size("spec")
    links = [(k, k + 1) for k in range(1, geo - 1, 2)]
    cores = [(k, k + 1) for k in range(0, geo, 2)]
    east = [(k, k + 1) for k in range(spec - 1)]
    both = lambda pairs: pairs + [(b, a) for a, b in pairs]
    return (
        lax.ppermute(cross, "geo", both(links)),
        lax.ppermute(chip, "geo", both(cores)),
        lax.ppermute(side, "spec", east),
        lax.ppermute(side, "spec", [(b, a) for a, b in east]),
    )


def per_device(
    spectrum, wind_speed, wind_dir, current_u, current_v, refract_x, refract_y, land_mask
):
    rows = spectrum.shape[0] * spectrum.shape[1] * spectrum.shape[2]
    flat = spectrum.reshape(rows, LANES)
    energy, cross, chip, side = pl.pallas_call(
        source_kernel,
        out_shape=packets(),
        in_specs=[ANY] + [VMEM] * 5,
        out_specs=[VMEM] * 4,
        scratch_shapes=[pltpu.VMEM((PADF * 2 * ND, LANES), F32), pltpu.SemaphoreType.DMA],
        compiler_params=PARAMS,
        name="source",
    )(flat, wind_speed, wind_dir, current_u, current_v, land_mask)
    halo = exchange(cross, chip, side)
    energy, cross, chip, side = pl.pallas_call(
        functools.partial(transport_kernel, False),
        out_shape=packets(),
        in_specs=[VMEM] * 10,
        out_specs=[VMEM] * 4,
        scratch_shapes=[pltpu.VMEM((2 * ND, LANES), F32)],
        compiler_params=PARAMS,
        name="first_substep",
    )(energy, *halo, current_u, current_v, refract_x, refract_y, land_mask)
    halo = exchange(cross, chip, side)
    out = pl.pallas_call(
        functools.partial(transport_kernel, True),
        out_shape=jax.ShapeDtypeStruct((rows, LANES), F32),
        in_specs=[VMEM] * 10,
        out_specs=ANY,
        scratch_shapes=[
            pltpu.VMEM((PADF * 2 * ND, LANES), F32),
            pltpu.VMEM((2 * ND, LANES), F32),
            pltpu.SemaphoreType.DMA,
        ],
        compiler_params=PARAMS,
        name="second_substep",
    )(energy, *halo, current_u, current_v, refract_x, refract_y, land_mask)
    return out.reshape(spectrum.shape)


def solution(mesh):
    in_specs = (
        P(None, None, "geo", "spec"),
        P("geo", "spec"),
        P("geo", "spec"),
        P("geo", None),
        P("geo", None),
        P("geo", None),
        P("geo", None),
        P("geo", None),
    )
    out_specs = P(None, None, "geo", "spec")
    return jax.shard_map(
        per_device, mesh=mesh, in_specs=in_specs, out_specs=out_specs, check_vma=False
    )
```

profile of v0, /device:TPU:128, one launch (start us, length us, event | category | flops | bytes accessed | tf_op | source)
XLA Modules:
  0.0 56.1 jit_solution(7695655946820544672)
XLA Ops:
  0.0 0.0 copy-start
  0.0 1.5 %copy-done = f32[50,36,2,128]{3,2,1,0:T(2,128)S(1)} copy-done((f32[50,36,2,128]{3,2,1,0:T(2,128)S(1)}, f32[50,36,2,128]{3,2,1,0:T(2,128)}, u32[]{:S(2)}) %copy-start) | copy-done | bytes 1843224
  1.5 0.0 copy-start.1
  1.5 0.7 %copy-done.1 = f32[2,512]{1,0:T(2,128)S(1)} copy-done((f32[2,512]{1,0:T(2,128)S(1)}, f32[2,512]{1,0:T(2,128)}, u32[]{:S(2)}) %copy-start.1) | copy-done | bytes 4120
  2.2 0.0 copy-start.2
  2.2 0.7 %copy-done.2 = f32[2,512]{1,0:T(2,128)S(1)} copy-done((f32[2,512]{1,0:T(2,128)S(1)}, f32[2,512]{1,0:T(2,128)}, u32[]{:S(2)}) %copy-start.2) | copy-done | bytes 4120
  2.9 0.0 copy-start.3
  2.9 0.7 %copy-done.3 = s32[2,512]{1,0:T(2,128)S(1)} copy-done((s32[2,512]{1,0:T(2,128)S(1)}, s32[2,512]{1,0:T(2,128)}, u32[]{:S(2)}) %copy-start.3) | copy-done | bytes 4120
  3.6 0.0 copy-start.8
  3.6 0.7 %copy-done.8 = f32[2,128]{1,0:T(2,128)S(1)} copy-done((f32[2,128]{1,0:T(2,128)S(1)}, f32[2,128]{1,0:T(2,128)}, u32[]{:S(2)}) %copy-start.8) | copy-done | bytes 1048
  4.2 0.0 copy-start.9
  4.2 0.7 %copy-done.9 = f32[2,128]{1,0:T(2,128)S(1)} copy-done((f32[2,128]{1,0:T(2,128)S(1)}, f32[2,128]{1,0:T(2,128)}, u32[]{:S(2)}) %copy-start.9) | copy-done | bytes 1048
  4.9 2.7 %source.1 = (f32[4032,128]{1,0:T(8,128)S(1)}, f32[1624,128]{1,0:T(8,128)S(1)}, f32[1624,128]{1,0:T(8,128)S(1)}, f32[112,128]{1,0:T(8,128)S(1)}) custom-call(f32[3600,128]{1,0:T(8,128)S(1)} %bitcast.2, f32[2,128]{1,0:T(2,128)S(1)} %copy-done.8, f32[2,128]{1,0:T(2,128)S(1)} %copy-done.9, f32[2,512]{1,0:T(2,128)S(1)} %copy-done.1, f32[2,512]{1,0:T(2,128)S(1)} %copy-done.2, ...), custom_call_target="tpu_custom_call" | custom-call | tf_op jit(solution)/shard_map/source/pallas_call | solution.py:319
  7.6 0.0 copy-start.6
  7.6 3.9 %collective-permute-start = (f32[1624,128]{1,0:T(8,128)S(1)}, f32[1624,128]{1,0:T(8,128)S(1)}, u32[]{:S(2)}, u32[]{:S(2)}) collective-permute-start(f32[1624,128]{1,0:T(8,128)S(1)} %get-tuple-element.14), channel_id=1, source_target_pairs={{4,8},{12,16},{20,24},{28,32},{36,40},{44,48},{52,56},{60,64},{68,... | collective-permute-start | bytes 2494472 | tf_op jit(solution)/shard_map/ppermute | solution.py:307
  11.5 0.1 collective-permute-start.1
  11.6 1.3 %collective-permute-start.3 = (f32[112,128]{1,0:T(8,128)S(1)}, f32[112,128]{1,0:T(8,128)S(1)}, u32[]{:S(2)}, u32[]{:S(2)}) collective-permute-start(f32[112,128]{1,0:T(8,128)S(1)} %get-tuple-element.16), channel_id=1, source_target_pairs={{1,0},{2,1},{3,2},{5,4},{6,5},{7,6},{9,8},{10,9},{11,10},{13,12},{... | collective-permute-start | bytes 172040 | tf_op jit(solution)/shard_map/ppermute | solution.py:310
  12.9 4.5 %collective-permute-start.2 = (f32[112,128]{1,0:T(8,128)S(1)}, f32[112,128]{1,0:T(8,128)S(1)}, u32[]{:S(2)}, u32[]{:S(2)}) collective-permute-start(f32[112,128]{1,0:T(8,128)S(1)} %get-tuple-element.16), channel_id=1, source_target_pairs={{0,1},{1,2},{2,3},{4,5},{5,6},{6,7},{8,9},{9,10},{10,11},{12,13},{... | collective-permute-start | bytes 172040 | tf_op jit(solution)/shard_map/ppermute | solution.py:309
  17.5 0.3 collective-permute-done.3.east_in
  17.8 1.5 %collective-permute-done.2.west_in = f32[112,128]{1,0:T(8,128)S(1)} collective-permute-done((f32[112,128]{1,0:T(8,128)S(1)}, f32[112,128]{1,0:T(8,128)S(1)}, u32[]{:S(2)}, u32[]{:S(2)}) %collective-permute-start.2) | collective-permute-done | bytes 57376 | tf_op jit(solution)/shard_map/ppermute | solution.py:309
  19.3 5.4 %collective-permute-done.cross_in = f32[1624,128]{1,0:T(8,128)S(1)} collective-permute-done((f32[1624,128]{1,0:T(8,128)S(1)}, f32[1624,128]{1,0:T(8,128)S(1)}, u32[]{:S(2)}, u32[]{:S(2)}) %collective-permute-start) | collective-permute-done | bytes 831520 | tf_op jit(solution)/shard_map/ppermute | solution.py:307
  24.7 0.0 collective-permute-done.1.chip_in
  24.7 0.0 copy-start.4
  24.7 0.7 %copy-done.4 = s32[2,512]{1,0:T(2,128)S(1)} copy-done((s32[2,512]{1,0:T(2,128)S(1)}, s32[2,512]{1,0:T(2,128)}, u32[]{:S(2)}) %copy-start.4) | copy-done | bytes 4120
  25.4 0.0 copy-start.5
  25.4 0.7 %copy-done.5 = f32[2,512]{1,0:T(2,128)S(1)} copy-done((f32[2,512]{1,0:T(2,128)S(1)}, f32[2,512]{1,0:T(2,128)}, u32[]{:S(2)}) %copy-start.5) | copy-done | bytes 4120
  26.1 0.0 copy-start.7
  26.1 0.7 %copy-done.7 = f32[2,512]{1,0:T(2,128)S(1)} copy-done((f32[2,512]{1,0:T(2,128)S(1)}, f32[2,512]{1,0:T(2,128)}, u32[]{:S(2)}) %copy-start.7) | copy-done | bytes 4120
  26.8 8.3 %first_substep.1 = (f32[4032,128]{1,0:T(8,128)S(1)}, f32[1624,128]{1,0:T(8,128)S(1)}, f32[1624,128]{1,0:T(8,128)S(1)}, f32[112,128]{1,0:T(8,128)S(1)}) custom-call(f32[4032,128]{1,0:T(8,128)S(1)} %get-tuple-element.13.e_ref, f32[1624,128]{1,0:T(8,128)S(1)} %collective-permute-done.cross_in, f32[1624,128]{1,0:T(8,128)S(1)} %collective-permute-done.1.chip_in, ...), custom_call_target="tpu_custom_call" | custom-call | tf_op jit(solution)/shard_map/first_substep/pallas_call | solution.py:329
  35.1 3.9 %collective-permute-start.4 = (f32[1624,128]{1,0:T(8,128)S(1)}, f32[1624,128]{1,0:T(8,128)S(1)}, u32[]{:S(2)}, u32[]{:S(2)}) collective-permute-start(f32[1624,128]{1,0:T(8,128)S(1)} %get-tuple-element.18), channel_id=1, source_target_pairs={{4,8},{12,16},{20,24},{28,32},{36,40},{44,48},{52,56},{60,64},{68,... | collective-permute-start | bytes 2494472 | tf_op jit(solution)/shard_map/ppermute | solution.py:307
  39.0 0.1 collective-permute-start.5
  39.1 1.3 %collective-permute-start.7 = (f32[112,128]{1,0:T(8,128)S(1)}, f32[112,128]{1,0:T(8,128)S(1)}, u32[]{:S(2)}, u32[]{:S(2)}) collective-permute-start(f32[112,128]{1,0:T(8,128)S(1)} %get-tuple-element.20), channel_id=1, source_target_pairs={{1,0},{2,1},{3,2},{5,4},{6,5},{7,6},{9,8},{10,9},{11,10},{13,12},{... | collective-permute-start | bytes 172040 | tf_op jit(solution)/shard_map/ppermute | solution.py:310
  40.4 4.5 %collective-permute-start.6 = (f32[112,128]{1,0:T(8,128)S(1)}, f32[112,128]{1,0:T(8,128)S(1)}, u32[]{:S(2)}, u32[]{:S(2)}) collective-permute-start(f32[112,128]{1,0:T(8,128)S(1)} %get-tuple-element.20), channel_id=1, source_target_pairs={{0,1},{1,2},{2,3},{4,5},{5,6},{6,7},{8,9},{9,10},{10,11},{12,13},{... | collective-permute-start | bytes 172040 | tf_op jit(solution)/shard_map/ppermute | solution.py:309
  45.0 0.3 collective-permute-done.7.east_in
  45.3 1.5 %collective-permute-done.6.west_in = f32[112,128]{1,0:T(8,128)S(1)} collective-permute-done((f32[112,128]{1,0:T(8,128)S(1)}, f32[112,128]{1,0:T(8,128)S(1)}, u32[]{:S(2)}, u32[]{:S(2)}) %collective-permute-start.6) | collective-permute-done | bytes 57376 | tf_op jit(solution)/shard_map/ppermute | solution.py:309
  46.8 5.4 %collective-permute-done.4.cross_in = f32[1624,128]{1,0:T(8,128)S(1)} collective-permute-done((f32[1624,128]{1,0:T(8,128)S(1)}, f32[1624,128]{1,0:T(8,128)S(1)}, u32[]{:S(2)}, u32[]{:S(2)}) %collective-permute-start.4) | collective-permute-done | bytes 831520 | tf_op jit(solution)/shard_map/ppermute | solution.py:307
  52.2 0.0 collective-permute-done.5.chip_in
  52.2 0.0 copy-done.6
  52.2 3.9 %second_substep.1 = f32[3600,128]{1,0:T(8,128)} custom-call(f32[4032,128]{1,0:T(8,128)S(1)} %get-tuple-element.17.e_ref, f32[1624,128]{1,0:T(8,128)S(1)} %collective-permute-done.4.cross_in, f32[1624,128]{1,0:T(8,128)S(1)} %collective-permute-done.5.chip_in, f32[112,128]{1,0:T(8,128)S(1)} %collective-permute-done.6.west_in, ...), custom_call_target="tpu_custom_call" | custom-call | tf_op jit(solution)/shard_map/second_substep/pallas_call | solution.py:339
Async XLA Ops:
  0.0 1.5 %copy-start = (f32[50,36,2,128]{3,2,1,0:T(2,128)S(1)}, f32[50,36,2,128]{3,2,1,0:T(2,128)}, u32[]{:S(2)}) copy-start(f32[50,36,2,128]{3,2,1,0:T(2,128)} %param.8) | copy-start | bytes 5529604
  1.5 0.7 %copy-start.1 = (f32[2,512]{1,0:T(2,128)S(1)}, f32[2,512]{1,0:T(2,128)}, u32[]{:S(2)}) copy-start(f32[2,512]{1,0:T(2,128)} %u_ref.5) | copy-start | bytes 12292
  2.2 0.7 %copy-start.2 = (f32[2,512]{1,0:T(2,128)S(1)}, f32[2,512]{1,0:T(2,128)}, u32[]{:S(2)}) copy-start(f32[2,512]{1,0:T(2,128)} %v_ref.5) | copy-start | bytes 12292
  2.9 0.7 %copy-start.3 = (s32[2,512]{1,0:T(2,128)S(1)}, s32[2,512]{1,0:T(2,128)}, u32[]{:S(2)}) copy-start(s32[2,512]{1,0:T(2,128)} %sea_ref.5) | copy-start | bytes 12292
  3.6 0.7 %copy-start.8 = (f32[2,128]{1,0:T(2,128)S(1)}, f32[2,128]{1,0:T(2,128)}, u32[]{:S(2)}) copy-start(f32[2,128]{1,0:T(2,128)} %ws_ref.1) | copy-start | bytes 3076
  4.2 0.7 %copy-start.9 = (f32[2,128]{1,0:T(2,128)S(1)}, f32[2,128]{1,0:T(2,128)}, u32[]{:S(2)}) copy-start(f32[2,128]{1,0:T(2,128)} %wd_ref.1) | copy-start | bytes 3076
  7.6 44.6 %copy-start.6 = (f32[2,512]{1,0:T(2,128)S(1)}, f32[2,512]{1,0:T(2,128)}, u32[]{:S(2)}) copy-start(f32[2,512]{1,0:T(2,128)} %rx_ref.3) | copy-start | bytes 12292
  7.6 17.1 %collective-permute-start = (f32[1624,128]{1,0:T(8,128)S(1)}, f32[1624,128]{1,0:T(8,128)S(1)}, u32[]{:S(2)}, u32[]{:S(2)}) collective-permute-start(f32[1624,128]{1,0:T(8,128)S(1)} %get-tuple-element.14), channel_id=1, source_target_pairs={{4,8},{12,16},{20,24},{28,32},{36,40},{44,48},{52,56},{60,64},{68,... | collective-permute-start | bytes 2494472 | tf_op jit(solution)/shard_map/ppermute | solution.py:307
  11.5 13.2 %collective-permute-start.1 = (f32[1624,128]{1,0:T(8,128)S(1)}, f32[1624,128]{1,0:T(8,128)S(1)}, u32[]{:S(2)}, u32[]{:S(2)}) collective-permute-start(f32[1624,128]{1,0:T(8,128)S(1)} %get-tuple-element.15), channel_id=1, source_target_pairs={{0,4},{8,12},{16,20},{24,28},{32,36},{40,44},{48,52},{56,60},{64,6... | collective-permute-start | bytes 2494472 | tf_op jit(solution)/shard_map/ppermute | solution.py:308
  11.6 6.2 %collective-permute-start.3 = (f32[112,128]{1,0:T(8,128)S(1)}, f32[112,128]{1,0:T(8,128)S(1)}, u32[]{:S(2)}, u32[]{:S(2)}) collective-permute-start(f32[112,128]{1,0:T(8,128)S(1)} %get-tuple-element.16), channel_id=1, source_target_pairs={{1,0},{2,1},{3,2},{5,4},{6,5},{7,6},{9,8},{10,9},{11,10},{13,12},{... | collective-permute-start | bytes 172040 | tf_op jit(solution)/shard_map/ppermute | solution.py:310
  12.9 6.4 %collective-permute-start.2 = (f32[112,128]{1,0:T(8,128)S(1)}, f32[112,128]{1,0:T(8,128)S(1)}, u32[]{:S(2)}, u32[]{:S(2)}) collective-permute-start(f32[112,128]{1,0:T(8,128)S(1)} %get-tuple-element.16), channel_id=1, source_target_pairs={{0,1},{1,2},{2,3},{4,5},{5,6},{6,7},{8,9},{9,10},{10,11},{12,13},{... | collective-permute-start | bytes 172040 | tf_op jit(solution)/shard_map/ppermute | solution.py:309
  24.7 0.7 %copy-start.4 = (s32[2,512]{1,0:T(2,128)S(1)}, s32[2,512]{1,0:T(2,128)}, u32[]{:S(2)}) copy-start(s32[2,512]{1,0:T(2,128)} %sea_ref.5) | copy-start | bytes 12292
  25.4 0.7 %copy-start.5 = (f32[2,512]{1,0:T(2,128)S(1)}, f32[2,512]{1,0:T(2,128)}, u32[]{:S(2)}) copy-start(f32[2,512]{1,0:T(2,128)} %rx_ref.3) | copy-start | bytes 12292
  26.1 0.7 %copy-start.7 = (f32[2,512]{1,0:T(2,128)S(1)}, f32[2,512]{1,0:T(2,128)}, u32[]{:S(2)}) copy-start(f32[2,512]{1,0:T(2,128)} %ry_ref.3) | copy-start | bytes 12292
  35.1 17.1 %collective-permute-start.4 = (f32[1624,128]{1,0:T(8,128)S(1)}, f32[1624,128]{1,0:T(8,128)S(1)}, u32[]{:S(2)}, u32[]{:S(2)}) collective-permute-start(f32[1624,128]{1,0:T(8,128)S(1)} %get-tuple-element.18), channel_id=1, source_target_pairs={{4,8},{12,16},{20,24},{28,32},{36,40},{44,48},{52,56},{60,64},{68,... | collective-permute-start | bytes 2494472 | tf_op jit(solution)/shard_map/ppermute | solution.py:307
  39.0 13.2 %collective-permute-start.5 = (f32[1624,128]{1,0:T(8,128)S(1)}, f32[1624,128]{1,0:T(8,128)S(1)}, u32[]{:S(2)}, u32[]{:S(2)}) collective-permute-start(f32[1624,128]{1,0:T(8,128)S(1)} %get-tuple-element.19), channel_id=1, source_target_pairs={{0,4},{8,12},{16,20},{24,28},{32,36},{40,44},{48,52},{56,60},{64,6... | collective-permute-start | bytes 2494472 | tf_op jit(solution)/shard_map/ppermute | solution.py:308
  39.1 6.2 %collective-permute-start.7 = (f32[112,128]{1,0:T(8,128)S(1)}, f32[112,128]{1,0:T(8,128)S(1)}, u32[]{:S(2)}, u32[]{:S(2)}) collective-permute-start(f32[112,128]{1,0:T(8,128)S(1)} %get-tuple-element.20), channel_id=1, source_target_pairs={{1,0},{2,1},{3,2},{5,4},{6,5},{7,6},{9,8},{10,9},{11,10},{13,12},{... | collective-permute-start | bytes 172040 | tf_op jit(solution)/shard_map/ppermute | solution.py:310
  40.4 6.4 %collective-permute-start.6 = (f32[112,128]{1,0:T(8,128)S(1)}, f32[112,128]{1,0:T(8,128)S(1)}, u32[]{:S(2)}, u32[]{:S(2)}) collective-permute-start(f32[112,128]{1,0:T(8,128)S(1)} %get-tuple-element.20), channel_id=1, source_target_pairs={{0,1},{1,2},{2,3},{4,5},{5,6},{6,7},{8,9},{9,10},{10,11},{12,13},{... | collective-permute-start | bytes 172040 | tf_op jit(solution)/shard_map/ppermute | solution.py:309
where the time goes:
time: 56.6 us; the launch traced here: 56.1 us
  starting transfers between devices  19.7 us (35%)
  Pallas kernels  14.9 us (26%)
  waiting for transfers between devices  14.5 us (26%)
  local copies, waits for them, and re-layouts  6.98 us (12%)
    ppermute x2, waiting for transfers between devices, exchange(): lax.ppermute(cross, 'geo', both(links))  10.9 us
    ppermute x2, starting transfers between devices, exchange(): lax.ppermute(side, 'spec', east)  9.1 us
    pallas_call x1, Pallas kernels, per_device(): pl.pallas_call(functools.partial(transport_kernel, False), out_shape=pack...  8.3 us
    ppermute x2, starting transfers between devices, exchange(): lax.ppermute(cross, 'geo', both(links))  7.81 us
    unnamed x20, local copies, waits for them, and re-layouts  6.98 us
    pallas_call x1, Pallas kernels, per_device(): pl.pallas_call(functools.partial(transport_kernel, True), out_shape=jax.S...  3.9 us
    ppermute x2, waiting for transfers between devices, exchange(): lax.ppermute(side, 'spec', east)  2.93 us
    pallas_call x1, Pallas kernels, per_device(): pl.pallas_call(source_kernel, out_shape=packets(), in_specs=[ANY] + [VMEM...  2.67 us
  transfers between devices with their start and end apart: 8, of which 6 were waited for; matrix products, arithmetic and copies ran while one was open for 0% of the time, Pallas kernels for 0%

commit v1 on v0

v1 whole, which is shorter than its diff:
```python
import functools
import math

import jax
import jax.numpy as jnp
from jax import lax
from jax.experimental import pallas as pl
from jax.experimental.pallas import tpu as pltpu
from jax.sharding import PartitionSpec as P

gravity = 9.81
lowest_radian = 2.0 * math.pi * 0.0373
log_span = 49.0 * math.log(1.1)
wind_coef = 1.7e-06
break_coef = 2.5e-05
steep_ref = 480.0
wind_factor = 1.1
source_seconds = 360.0
courant_cells = 0.02
substep_seconds = 180.0

NF = 50
ND = 36
LANES = 128
SUB = 8
GROUPS = 7
PADF = SUB * GROUPS
RATIO = log_span / (NF - 1)
DTH = 2.0 * math.pi / ND
COS = [math.cos(DTH * i) for i in range(ND)]
SIN = [math.sin(DTH * i) for i in range(ND)]
GSPEED = [gravity / (2.0 * lowest_radian * math.exp(RATIO * j)) for j in range(NF)]
FIRST = [
    min(j for j in range(NF) if GSPEED[j] * SIN[i] > -1.001) // SUB for i in range(ND)
]
RANK = [0] * ND
for place, i_of in enumerate(sorted(range(ND), key=lambda i: (FIRST[i], i))):
    RANK[i_of] = place
COUNT = [sum(1 for i in range(ND) if FIRST[i] <= g) for g in range(GROUPS)]
BASE = [SUB * sum(COUNT[:g]) for g in range(GROUPS)]
TAIL = NF - SUB * (GROUPS - 1)
FIT = SUB // TAIL
SPARE = BASE[-1] + SUB * (ND // FIT)
PACKET = SPARE + SUB
TURN = 8
FIELDS = TURN + 2 * ND
BATCH = 3
CHUNK = SUB * 2 * ND
FIELD = 2 * ND * PADF
SIDE = 2 * PADF
F32 = jnp.float32


def mirrored(i):
    return (ND - i) % ND


LAST = GROUPS - 1


def group_base(group):
    if group is LAST:
        return BASE[-1]
    total = 0
    for g in range(GROUPS - 1):
        total = total + jnp.where(group > g, SUB * COUNT[g], 0)
    return total


def slot(base, group, i):
    place = base + SUB * RANK[i]
    if FIRST[i] > 0:
        place = jnp.where(group >= FIRST[i], place, SPARE)
    return aligned(place)


def aligned(start):
    return pl.ds(start if isinstance(start, int) else pl.multiple_of(start, SUB), SUB)


def field_rows(group, r, i):
    return aligned((r * ND + i) * PADF + group * SUB)


def side_rows(group, r):
    return aligned(r * PADF + group * SUB)


def fetch(ref, group, base, i):
    if group is LAST:
        got = ref[aligned(BASE[-1] + SUB * (RANK[i] // FIT)), :]
        return pltpu.roll(got, (SUB - TAIL * (RANK[i] % FIT)) % SUB, 0)
    return ref[slot(base, group, i), :]


class Sender:
    def __init__(self, ref, group, base):
        self.ref, self.group, self.base, self.shared = ref, group, base, {}

    def put(self, i, value):
        if self.group is not LAST:
            return [(self.ref, slot(self.base, self.group, i), value)]
        block, part = RANK[i] // FIT, RANK[i] % FIT
        held = self.shared.setdefault(block, {})
        held[part] = pltpu.roll(value, TAIL * part, 0) if part else value
        if len(held) < FIT:
            return []
        place = lax.broadcasted_iota(jnp.int32, (SUB, LANES), 0)
        full = held[FIT - 1]
        for part in range(FIT - 1):
            inside = (place >= TAIL * part) & (place < TAIL * (part + 1))
            full = jnp.where(inside, held[part], full)
        return [(self.ref, aligned(BASE[-1] + SUB * block), full)]


def radian_of(group):
    j = lax.broadcasted_iota(jnp.int32, (SUB, LANES), 0) + group * SUB
    return lowest_radian * jnp.exp(j.astype(F32) * RATIO), j


def position():
    odd = lax.rem(lax.axis_index("geo"), 2)
    col = pl.multiple_of(lax.axis_index("spec") * LANES, LANES)
    sign = jnp.where(odd == 1, -1.0, 1.0).astype(F32)
    return odd, col, sign


def row_of(ref, odd, r, col):
    window = (ref[...] if col is None else ref[:, pl.ds(col, LANES)]).astype(F32)
    first, second = window[0:1], window[1:2]
    own, other = (first, second) if r == 0 else (second, first)
    return jnp.where(odd == 1, other, own)


def spread(row):
    return jnp.broadcast_to(row, (SUB, LANES))


def lane_ids():
    return lax.broadcasted_iota(jnp.int32, (SUB, LANES), 1)


class Gather:
    def __init__(self, lane):
        self.lane, self.pair = lane, lax.shift_right_logical(lane + 1, 1)
        self.total = [jnp.zeros((SUB, LANES), F32)] * 2
        self.queue = []

    def put(self, i, energy, cx):
        flux = []
        for r in range(2):
            speed = jnp.where(self.lane == 0, jnp.minimum(cx[r], 0.0), jnp.maximum(cx[r], 0.0))
            flux.append(speed * energy[r])
        self.queue.append((i, flux))

    def finish(self, side_ref, group):
        for i, flux in self.queue:
            for r in range(2):
                moved = pltpu.roll(flux[r], 2 * i + 2, 1)
                self.total[r] = jnp.where(self.pair == i + 1, moved, self.total[r])
        for r in range(2):
            side_ref[side_rows(group, r), :] = self.total[r]


def emit(i, energy, cx, cy, gather, cross, chip):
    gather.put(i, energy, cx)
    stores = cross.put(mirrored(i), jnp.maximum(-cy[0], 0.0) * energy[0])
    return stores + chip.put(i, jnp.maximum(cy[1], 0.0) * energy[1])


def flush(stores):
    for ref, rows, value in stores:
        ref[rows, :] = value
    stores.clear()


def each_group(body):
    lax.fori_loop(0, LAST, lambda group, carry: body(group) or carry, 0)
    body(LAST)


def finish_packets(cross_ref, chip_ref):
    blank = jnp.zeros((SUB, LANES), F32)
    cross_ref[SPARE:PACKET, :] = blank
    chip_ref[SPARE:PACKET, :] = blank


def source_kernel(*refs):
    inputs, refs = refs[:8], refs[8:]
    e_ref, cross_ref, chip_ref, side_ref, fields_ref, raw = refs[:6]
    held, sems = refs[6:13], refs[13]
    odd, col, sign = position()
    copies = [
        pltpu.make_async_copy(source, target, sems.at[GROUPS + k])
        for k, (source, target) in enumerate(zip(inputs[1:], held))
    ]

    def chunk(group, size):
        rows = pl.ds(group * CHUNK, size)
        return pltpu.make_async_copy(inputs[0].at[rows], raw.at[rows], sems.at[group])

    final = chunk(LAST, TAIL * 2 * ND)
    for group in range(LAST):
        chunk(group, CHUNK).start()
    final.start()
    for copy in copies:
        copy.start()
    raw[NF * 2 * ND :, :] = jnp.zeros(((PADF - NF) * 2 * ND, LANES), F32)
    ws_ref, wd_ref, u_ref, v_ref, rx_ref, ry_ref, sea_ref = held

    def stats(group, sums):
        if group is LAST:
            final.wait()
        else:
            chunk(group, CHUNK).wait()
        s, j = radian_of(group)
        valid = j < NF
        w1 = jnp.where(valid, s * ((math.exp(RATIO) - 1.0) * DTH), 0.0)
        w2 = jnp.where(valid, (math.exp(RATIO) - 1.0) * DTH, 0.0)
        out = []
        for r in range(2):
            parts = [None, None, None, None]
            r_from = jnp.where(odd == 1, 1 - r, r)
            stores = []
            for i in range(ND):
                i_from = jnp.where(odd == 1, 2 * mirrored(i), 2 * i)
                got = raw[pl.ds(group * CHUNK + i_from + r_from, SUB, stride=2 * ND), :]
                stores.append((e_ref, field_rows(group, r, i), got))
                k = i % 4
                parts[k] = got if parts[k] is None else parts[k] + got
                if i % 9 == 8:
                    flush(stores)
            part = (parts[0] + parts[1]) + (parts[2] + parts[3])
            out.append((sums[r][0] + part * w1, sums[r][1] + part * w2))
        return tuple(out)

    blank = jnp.zeros((SUB, LANES), F32)
    sums = stats(LAST, lax.fori_loop(0, LAST, stats, ((blank, blank), (blank, blank))))
    for copy in copies:
        copy.wait()
    wind_x, wind_y, sea, decay, u, v = [], [], [], [], [], []
    for r in range(2):
        total = jnp.sum(sums[r][0], axis=0, keepdims=True)
        inverse = jnp.sum(sums[r][1], axis=0, keepdims=True)
        mean_sigma = total / inverse
        mean_k = mean_sigma * mean_sigma / gravity
        ratio = total * mean_k * mean_k / steep_ref
        decay.append(spread(source_seconds * break_coef * ratio * ratio / mean_sigma))
        strength = row_of(ws_ref, odd, r, None) * (wind_factor / gravity)
        angle = row_of(wd_ref, odd, r, None) * sign
        wind_x.append(spread(strength * jnp.cos(angle)))
        wind_y.append(spread(strength * jnp.sin(angle)))
        own = [
            row_of(sea_ref, odd, r, col),
            courant_cells * row_of(u_ref, odd, r, col),
            courant_cells * sign * row_of(v_ref, odd, r, col),
        ]
        for k in range(3):
            fields_ref[2 * k + r : 2 * k + r + 1, :] = own[k]
        sea.append(spread(own[0]))
        u.append(spread(own[1]))
        v.append(spread(own[2]))
        rx = row_of(rx_ref, odd, r, col)
        ry = sign * row_of(ry_ref, odd, r, col)
        for i in range(ND):
            at = TURN + r * ND + i
            fields_ref[at : at + 1, :] = SIN[i] * rx - COS[i] * ry
    lane = lane_ids()

    def source(group):
        s, _ = radian_of(group)
        fc = (courant_cells * gravity / 2.0) / s
        gain = s * (source_seconds * wind_coef)
        damp = [sea[r] / (1.0 + decay[r] * s * s) for r in range(2)]
        base = group_base(group)
        cross, chip = Sender(cross_ref, group, base), Sender(chip_ref, group, base)
        gather, stores = Gather(lane), []
        for i in range(ND):
            energy, cx, cy = [], [], []
            for r in range(2):
                rows = field_rows(group, r, i)
                align = wind_x[r] * COS[i] + wind_y[r] * SIN[i]
                growth = gain * jnp.maximum(s * align - 1.0, 0.0)
                new = e_ref[rows, :] * damp[r] * (1.0 + growth)
                stores.append((e_ref, rows, new))
                energy.append(new)
                cx.append(fc * COS[i] + u[r])
                cy.append(fc * SIN[i] + v[r])
            stores += emit(i, energy, cx, cy, gather, cross, chip)
            if i % BATCH == BATCH - 1:
                flush(stores)
        gather.finish(side_ref, group)

    each_group(source)
    finish_packets(cross_ref, chip_ref)


def transport_kernel(last, e_ref, cross_in, chip_in, west_in, east_in, fields_ref, *rest):
    if last:
        out_hbm, work, sems = rest
    else:
        out_ref, cross_ref, chip_ref, side_ref = rest
    odd, _, _ = position()
    sea, u, v = [[spread(fields_ref[2 * k + r : 2 * k + r + 1, :]) for r in range(2)] for k in range(3)]
    lane = lane_ids()
    odd_lane = lax.rem(lane, 2) == 1
    blank = jnp.zeros((SUB, LANES), F32)

    def substep(group):
        s, _ = radian_of(group)
        c = (gravity / 2.0) / s
        fc = courant_cells * c
        tc = (substep_seconds / DTH) * c
        base = group_base(group)
        border = []
        for r in range(2):
            rows = side_rows(group, r)
            border.append(
                jnp.where(odd_lane, west_in[rows, :], pltpu.roll(east_in[rows, :], LANES - 2, 1))
            )

        def turned(r, i):
            energy = e_ref[field_rows(group, r, i), :]
            at = TURN + r * ND + i
            speed = tc * spread(fields_ref[at : at + 1, :])
            return energy, jnp.maximum(speed, 0.0) * energy, jnp.minimum(speed, 0.0) * energy

        before = [turned(r, ND - 1)[1] for r in range(2)]
        first = [turned(r, 0) for r in range(2)]
        here = first
        gather, stores = Gather(lane), []
        if not last:
            cross, chip = Sender(cross_ref, group, base), Sender(chip_ref, group, base)
        for i in range(ND):
            after = [turned(r, i + 1) for r in range(2)] if i + 1 < ND else first
            cx = [fc * COS[i] + u[r] for r in range(2)]
            cy = [fc * SIN[i] + v[r] for r in range(2)]
            energy = [here[r][0] for r in range(2)]
            py = [jnp.maximum(cy[r], 0.0) * energy[r] for r in range(2)]
            my = [jnp.minimum(cy[r], 0.0) * energy[r] for r in range(2)]
            from_cross = fetch(cross_in, group, base, i)
            from_chip = fetch(chip_in, group, base, mirrored(i))
            in_y = [from_cross - my[1], py[0] + from_chip]
            new = []
            for r in range(2):
                px = jnp.maximum(cx[r], 0.0) * energy[r]
                mx = jnp.minimum(cx[r], 0.0) * energy[r]
                brought = pltpu.roll(border[r], (LANES - (2 * i + 1)) % LANES, 1)
                px_in = jnp.where(lane == 0, brought, pltpu.roll(px, 1, 1))
                mx_in = jnp.where(lane == LANES - 1, brought, pltpu.roll(mx, LANES - 1, 1))
                stay = energy[r] - (px - mx) - (py[r] - my[r]) - (here[r][1] - here[r][2])
                gained = (px_in - mx_in) + in_y[r] + (before[r] - after[r][2])
                new.append(sea[r] * (stay + gained))
            for r in range(2):
                if last:
                    i_to = jnp.where(odd == 1, 2 * mirrored(i), 2 * i)
                    r_to = jnp.where(odd == 1, 1 - r, r)
                    start = group * CHUNK + i_to + r_to
                    stores.append((work, pl.ds(start, SUB, stride=2 * ND), new[r]))
                else:
                    stores.append((out_ref, field_rows(group, r, i), new[r]))
            if not last:
                stores += emit(i, new, cx, cy, gather, cross, chip)
            if i % BATCH == BATCH - 1:
                flush(stores)
            before = [here[r][1] for r in range(2)]
            here = after
        if not last:
            gather.finish(side_ref, group)

        if last:
            chunk(group).start()

    def chunk(group):
        rows = pl.ds(group * CHUNK, TAIL * 2 * ND if group is LAST else CHUNK)
        return pltpu.make_async_copy(work.at[rows], out_hbm.at[rows], sems.at[group])

    each_group(substep)
    if last:
        for group in range(LAST):
            chunk(group).wait()
        chunk(LAST).wait()
    else:
        finish_packets(cross_ref, chip_ref)


VMEM = pl.BlockSpec(memory_space=pltpu.VMEM)
HBM = pl.BlockSpec(memory_space=pltpu.HBM)
PARAMS = pltpu.CompilerParams(vmem_limit_bytes=24 * 1024 * 1024)


def shape(rows):
    return jax.ShapeDtypeStruct((rows, LANES), F32)


def packets():
    return [shape(FIELD), shape(PACKET), shape(PACKET), shape(SIDE)]


def exchange(cross, chip, side):
    geo, spec = lax.axis_size("geo"), lax.axis_size("spec")
    links = [(k, k + 1) for k in range(1, geo - 1, 2)]
    cores = [(k, k + 1) for k in range(0, geo, 2)]
    east = [(k, k + 1) for k in range(spec - 1)]
    both = lambda pairs: pairs + [(b, a) for a, b in pairs]
    return (
        lax.ppermute(cross, "geo", both(links)),
        lax.ppermute(chip, "geo", both(cores)),
        lax.ppermute(side, "spec", east),
        lax.ppermute(side, "spec", [(b, a) for a, b in east]),
    )


def per_device(
    spectrum, wind_speed, wind_dir, current_u, current_v, refract_x, refract_y, land_mask
):
    rows = spectrum.shape[0] * spectrum.shape[1] * spectrum.shape[2]
    flat = spectrum.reshape(rows, LANES)
    inputs = [flat, wind_speed, wind_dir, current_u, current_v, refract_x, refract_y, land_mask]
    inputs = [pltpu.with_memory_space_constraint(value, pltpu.HBM) for value in inputs]
    energy, cross, chip, side, fields = pl.pallas_call(
        source_kernel,
        out_shape=packets() + [shape(FIELDS)],
        in_specs=[HBM] * len(inputs),
        out_specs=[VMEM] * 5,
        scratch_shapes=[pltpu.VMEM((PADF * 2 * ND, LANES), F32)]
        + [pltpu.VMEM(value.shape, value.dtype) for value in inputs[1:]]
        + [pltpu.SemaphoreType.DMA((GROUPS + len(inputs) - 1,))],
        compiler_params=PARAMS,
        name="source",
    )(*inputs)
    halo = exchange(cross, chip, side)
    energy, cross, chip, side = pl.pallas_call(
        functools.partial(transport_kernel, False),
        out_shape=packets(),
        in_specs=[VMEM] * 6,
        out_specs=[VMEM] * 4,
        compiler_params=PARAMS,
        name="first_substep",
    )(energy, *halo, fields)
    halo = exchange(cross, chip, side)
    out = pl.pallas_call(
        functools.partial(transport_kernel, True),
        out_shape=shape(rows),
        in_specs=[VMEM] * 6,
        out_specs=HBM,
        scratch_shapes=[
            pltpu.VMEM((PADF * 2 * ND, LANES), F32),
            pltpu.SemaphoreType.DMA((GROUPS,)),
        ],
        compiler_params=PARAMS,
        name="second_substep",
    )(energy, *halo, fields)
    return out.reshape(spectrum.shape)


def solution(mesh):
    in_specs = (
        P(None, None, "geo", "spec"),
        P("geo", "spec"),
        P("geo", "spec"),
        P("geo", None),
        P("geo", None),
        P("geo", None),
        P("geo", None),
        P("geo", None),
    )
    out_specs = P(None, None, "geo", "spec")
    return jax.shard_map(
        per_device, mesh=mesh, in_specs=in_specs, out_specs=out_specs, check_vma=False
    )
```

time: 56.6 us -> 42.4 us (0.75)
  local copies, waits for them, and re-layouts: 6.98 us -> 0 us
  Pallas kernels: 14.9 us -> 10.2 us
  waiting for transfers between devices: 14.5 us -> 12.1 us
    unnamed x20 -> x0, local copies, waits for them, and re-layouts: 6.98 us -> none
    pallas_call x1, Pallas kernels: 8.3 us -> 3.3 us  [per_device(): pl.pallas_call(functools.partial(transport_kernel, False), out_shape=pack...]
    ppermute x2, waiting for transfers between devices: 10.9 us -> 8.49 us  [exchange(): lax.ppermute(cross, 'geo', both(links))]
where the time goes in v1:
time: 42.4 us; the launch traced here: 42.1 us
  starting transfers between devices  19.7 us (46%)
  waiting for transfers between devices  12.1 us (29%)
  Pallas kernels  10.2 us (24%)
    ppermute x2, starting transfers between devices, exchange(): lax.ppermute(side, 'spec', east)  9.1 us
    ppermute x2, waiting for transfers between devices, exchange(): lax.ppermute(cross, 'geo', both(links))  8.49 us
    ppermute x2, starting transfers between devices, exchange(): lax.ppermute(cross, 'geo', both(links))  7.81 us
    pallas_call x1, Pallas kernels, per_device(): pl.pallas_call(source_kernel, out_shape=packets() + [shape(FIELDS)], in_s...  3.6 us
    pallas_call x1, Pallas kernels, per_device(): pl.pallas_call(functools.partial(transport_kernel, True), out_shape=shape...  3.33 us
    pallas_call x1, Pallas kernels, per_device(): pl.pallas_call(functools.partial(transport_kernel, False), out_shape=pack...  3.3 us
    ppermute x2, waiting for transfers between devices, exchange(): lax.ppermute(side, 'spec', east)  2.93 us
    ppermute x2, starting transfers between devices, exchange(): lax.ppermute(side, 'spec', [(b, a) for a, b in east])  2.58 us
  transfers between devices with their start and end apart: 8, of which 6 were waited for; matrix products, arithmetic and copies ran while one was open for 0% of the time, Pallas kernels for 0%

profile of v1, /device:TPU:128, one launch (start us, length us, event | category | flops | bytes accessed | tf_op | source)
XLA Modules:
  0.0 42.1 jit_solution(695511210872808511)
XLA Ops:
  0.0 3.6 %source.1 = (f32[4032,128]{1,0:T(8,128)S(1)}, f32[1408,128]{1,0:T(8,128)S(1)}, f32[1408,128]{1,0:T(8,128)S(1)}, f32[112,128]{1,0:T(8,128)S(1)}, f32[80,128]{1,0:T(8,128)S(1)}) custom-call(f32[3600,128]{1,0:T(8,128)} %bitcast.2, f32[2,128]{1,0:T(2,128)} %refs_1_.1, f32[2,128]{1,0:T(2,128)} %refs_2_.1, f32[2,512]{1,0:T(2,128)} %refs_3_.1, f32[2,512]{1,0:T(2,128)} %refs_4_.1, ...), custom_call_target="tpu_custom_call" | custom-call | tf_op jit(solution)/shard_map/source/pallas_call | solution.py:421
  3.6 3.9 %collective-permute-start = (f32[1408,128]{1,0:T(8,128)S(1)}, f32[1408,128]{1,0:T(8,128)S(1)}, u32[]{:S(2)}, u32[]{:S(2)}) collective-permute-start(f32[1408,128]{1,0:T(8,128)S(1)} %get-tuple-element.15), channel_id=1, source_target_pairs={{4,8},{12,16},{20,24},{28,32},{36,40},{44,48},{52,56},{60,64},{68,... | collective-permute-start | bytes 2162696 | tf_op jit(solution)/shard_map/ppermute | solution.py:407
  7.5 0.1 collective-permute-start.1
  7.6 1.3 %collective-permute-start.3 = (f32[112,128]{1,0:T(8,128)S(1)}, f32[112,128]{1,0:T(8,128)S(1)}, u32[]{:S(2)}, u32[]{:S(2)}) collective-permute-start(f32[112,128]{1,0:T(8,128)S(1)} %get-tuple-element.17), channel_id=1, source_target_pairs={{1,0},{2,1},{3,2},{5,4},{6,5},{7,6},{9,8},{10,9},{11,10},{13,12},{... | collective-permute-start | bytes 172040 | tf_op jit(solution)/shard_map/ppermute | solution.py:410
  8.9 4.5 %collective-permute-start.2 = (f32[112,128]{1,0:T(8,128)S(1)}, f32[112,128]{1,0:T(8,128)S(1)}, u32[]{:S(2)}, u32[]{:S(2)}) collective-permute-start(f32[112,128]{1,0:T(8,128)S(1)} %get-tuple-element.17), channel_id=1, source_target_pairs={{0,1},{1,2},{2,3},{4,5},{5,6},{6,7},{8,9},{9,10},{10,11},{12,13},{... | collective-permute-start | bytes 172040 | tf_op jit(solution)/shard_map/ppermute | solution.py:409
  13.5 0.3 collective-permute-done.3.east_in
  13.8 1.5 %collective-permute-done.2.west_in = f32[112,128]{1,0:T(8,128)S(1)} collective-permute-done((f32[112,128]{1,0:T(8,128)S(1)}, f32[112,128]{1,0:T(8,128)S(1)}, u32[]{:S(2)}, u32[]{:S(2)}) %collective-permute-start.2) | collective-permute-done | bytes 57376 | tf_op jit(solution)/shard_map/ppermute | solution.py:409
  15.3 4.2 %collective-permute-done.cross_in = f32[1408,128]{1,0:T(8,128)S(1)} collective-permute-done((f32[1408,128]{1,0:T(8,128)S(1)}, f32[1408,128]{1,0:T(8,128)S(1)}, u32[]{:S(2)}, u32[]{:S(2)}) %collective-permute-start) | collective-permute-done | bytes 720928 | tf_op jit(solution)/shard_map/ppermute | solution.py:407
  19.5 0.0 collective-permute-done.1.chip_in
  19.5 3.3 %first_substep.1 = (f32[4032,128]{1,0:T(8,128)S(1)}, f32[1408,128]{1,0:T(8,128)S(1)}, f32[1408,128]{1,0:T(8,128)S(1)}, f32[112,128]{1,0:T(8,128)S(1)}) custom-call(f32[4032,128]{1,0:T(8,128)S(1)} %get-tuple-element.14.e_ref, f32[1408,128]{1,0:T(8,128)S(1)} %collective-permute-done.cross_in, f32[1408,128]{1,0:T(8,128)S(1)} %collective-permute-done.1.chip_in, ...), custom_call_target="tpu_custom_call" | custom-call | tf_op jit(solution)/shard_map/first_substep/pallas_call | solution.py:433
  22.8 3.9 %collective-permute-start.4 = (f32[1408,128]{1,0:T(8,128)S(1)}, f32[1408,128]{1,0:T(8,128)S(1)}, u32[]{:S(2)}, u32[]{:S(2)}) collective-permute-start(f32[1408,128]{1,0:T(8,128)S(1)} %get-tuple-element.20), channel_id=1, source_target_pairs={{4,8},{12,16},{20,24},{28,32},{36,40},{44,48},{52,56},{60,64},{68,... | collective-permute-start | bytes 2162696 | tf_op jit(solution)/shard_map/ppermute | solution.py:407
  26.8 0.1 collective-permute-start.5
  26.9 1.3 %collective-permute-start.7 = (f32[112,128]{1,0:T(8,128)S(1)}, f32[112,128]{1,0:T(8,128)S(1)}, u32[]{:S(2)}, u32[]{:S(2)}) collective-permute-start(f32[112,128]{1,0:T(8,128)S(1)} %get-tuple-element.22), channel_id=1, source_target_pairs={{1,0},{2,1},{3,2},{5,4},{6,5},{7,6},{9,8},{10,9},{11,10},{13,12},{... | collective-permute-start | bytes 172040 | tf_op jit(solution)/shard_map/ppermute | solution.py:410
  28.2 4.5 %collective-permute-start.6 = (f32[112,128]{1,0:T(8,128)S(1)}, f32[112,128]{1,0:T(8,128)S(1)}, u32[]{:S(2)}, u32[]{:S(2)}) collective-permute-start(f32[112,128]{1,0:T(8,128)S(1)} %get-tuple-element.22), channel_id=1, source_target_pairs={{0,1},{1,2},{2,3},{4,5},{5,6},{6,7},{8,9},{9,10},{10,11},{12,13},{... | collective-permute-start | bytes 172040 | tf_op jit(solution)/shard_map/ppermute | solution.py:409
  32.7 0.3 collective-permute-done.7.east_in
  33.1 1.5 %collective-permute-done.6.west_in = f32[112,128]{1,0:T(8,128)S(1)} collective-permute-done((f32[112,128]{1,0:T(8,128)S(1)}, f32[112,128]{1,0:T(8,128)S(1)}, u32[]{:S(2)}, u32[]{:S(2)}) %collective-permute-start.6) | collective-permute-done | bytes 57376 | tf_op jit(solution)/shard_map/ppermute | solution.py:409
  34.5 4.2 %collective-permute-done.4.cross_in = f32[1408,128]{1,0:T(8,128)S(1)} collective-permute-done((f32[1408,128]{1,0:T(8,128)S(1)}, f32[1408,128]{1,0:T(8,128)S(1)}, u32[]{:S(2)}, u32[]{:S(2)}) %collective-permute-start.4) | collective-permute-done | bytes 720928 | tf_op jit(solution)/shard_map/ppermute | solution.py:407
  38.8 0.0 collective-permute-done.5.chip_in
  38.8 3.3 %second_substep.1 = f32[3600,128]{1,0:T(8,128)} custom-call(f32[4032,128]{1,0:T(8,128)S(1)} %get-tuple-element.19.e_ref, f32[1408,128]{1,0:T(8,128)S(1)} %collective-permute-done.4.cross_in, f32[1408,128]{1,0:T(8,128)S(1)} %collective-permute-done.5.chip_in, f32[112,128]{1,0:T(8,128)S(1)} %collective-permute-done.6.west_in, ...), custom_call_target="tpu_custom_call" | custom-call | tf_op jit(solution)/shard_map/second_substep/pallas_call | solution.py:442
Async XLA Ops:
  3.6 15.9 %collective-permute-start = (f32[1408,128]{1,0:T(8,128)S(1)}, f32[1408,128]{1,0:T(8,128)S(1)}, u32[]{:S(2)}, u32[]{:S(2)}) collective-permute-start(f32[1408,128]{1,0:T(8,128)S(1)} %get-tuple-element.15), channel_id=1, source_target_pairs={{4,8},{12,16},{20,24},{28,32},{36,40},{44,48},{52,56},{60,64},{68,... | collective-permute-start | bytes 2162696 | tf_op jit(solution)/shard_map/ppermute | solution.py:407
  7.5 12.0 %collective-permute-start.1 = (f32[1408,128]{1,0:T(8,128)S(1)}, f32[1408,128]{1,0:T(8,128)S(1)}, u32[]{:S(2)}, u32[]{:S(2)}) collective-permute-start(f32[1408,128]{1,0:T(8,128)S(1)} %get-tuple-element.16), channel_id=1, source_target_pairs={{0,4},{8,12},{16,20},{24,28},{32,36},{40,44},{48,52},{56,60},{64,6... | collective-permute-start | bytes 2162696 | tf_op jit(solution)/shard_map/ppermute | solution.py:408
  7.6 6.2 %collective-permute-start.3 = (f32[112,128]{1,0:T(8,128)S(1)}, f32[112,128]{1,0:T(8,128)S(1)}, u32[]{:S(2)}, u32[]{:S(2)}) collective-permute-start(f32[112,128]{1,0:T(8,128)S(1)} %get-tuple-element.17), channel_id=1, source_target_pairs={{1,0},{2,1},{3,2},{5,4},{6,5},{7,6},{9,8},{10,9},{11,10},{13,12},{... | collective-permute-start | bytes 172040 | tf_op jit(solution)/shard_map/ppermute | solution.py:410
  8.9 6.4 %collective-permute-start.2 = (f32[112,128]{1,0:T(8,128)S(1)}, f32[112,128]{1,0:T(8,128)S(1)}, u32[]{:S(2)}, u32[]{:S(2)}) collective-permute-start(f32[112,128]{1,0:T(8,128)S(1)} %get-tuple-element.17), channel_id=1, source_target_pairs={{0,1},{1,2},{2,3},{4,5},{5,6},{6,7},{8,9},{9,10},{10,11},{12,13},{... | collective-permute-start | bytes 172040 | tf_op jit(solution)/shard_map/ppermute | solution.py:409
  22.8 15.9 %collective-permute-start.4 = (f32[1408,128]{1,0:T(8,128)S(1)}, f32[1408,128]{1,0:T(8,128)S(1)}, u32[]{:S(2)}, u32[]{:S(2)}) collective-permute-start(f32[1408,128]{1,0:T(8,128)S(1)} %get-tuple-element.20), channel_id=1, source_target_pairs={{4,8},{12,16},{20,24},{28,32},{36,40},{44,48},{52,56},{60,64},{68,... | collective-permute-start | bytes 2162696 | tf_op jit(solution)/shard_map/ppermute | solution.py:407
  26.8 12.0 %collective-permute-start.5 = (f32[1408,128]{1,0:T(8,128)S(1)}, f32[1408,128]{1,0:T(8,128)S(1)}, u32[]{:S(2)}, u32[]{:S(2)}) collective-permute-start(f32[1408,128]{1,0:T(8,128)S(1)} %get-tuple-element.21), channel_id=1, source_target_pairs={{0,4},{8,12},{16,20},{24,28},{32,36},{40,44},{48,52},{56,60},{64,6... | collective-permute-start | bytes 2162696 | tf_op jit(solution)/shard_map/ppermute | solution.py:408
  26.9 6.2 %collective-permute-start.7 = (f32[112,128]{1,0:T(8,128)S(1)}, f32[112,128]{1,0:T(8,128)S(1)}, u32[]{:S(2)}, u32[]{:S(2)}) collective-permute-start(f32[112,128]{1,0:T(8,128)S(1)} %get-tuple-element.22), channel_id=1, source_target_pairs={{1,0},{2,1},{3,2},{5,4},{6,5},{7,6},{9,8},{10,9},{11,10},{13,12},{... | collective-permute-start | bytes 172040 | tf_op jit(solution)/shard_map/ppermute | solution.py:410
  28.2 6.4 %collective-permute-start.6 = (f32[112,128]{1,0:T(8,128)S(1)}, f32[112,128]{1,0:T(8,128)S(1)}, u32[]{:S(2)}, u32[]{:S(2)}) collective-permute-start(f32[112,128]{1,0:T(8,128)S(1)} %get-tuple-element.22), channel_id=1, source_target_pairs={{0,1},{1,2},{2,3},{4,5},{5,6},{6,7},{8,9},{9,10},{10,11},{12,13},{... | collective-permute-start | bytes 172040 | tf_op jit(solution)/shard_map/ppermute | solution.py:409

commit v2 on v1

--- a/solution.py
+++ b/solution.py
@@ -123,6 +123,13 @@
     col = pl.multiple_of(lax.axis_index("spec") * LANES, LANES)
     sign = jnp.where(odd == 1, -1.0, 1.0).astype(F32)
     return odd, col, sign
+
+
+def inside():
+    geo, spec = lax.axis_index("geo"), lax.axis_index("spec")
+    first, last = lax.axis_size("geo") - 1, lax.axis_size("spec") - 1
+    keep = lambda edge: jnp.where(edge, 0.0, 1.0).astype(F32)
+    return keep((geo == 0) | (geo == first)), keep(spec == 0), keep(spec == last)
 
 
 def row_of(ref, odd, r, col):
@@ -301,6 +308,7 @@
     else:
         out_ref, cross_ref, chip_ref, side_ref = rest
     odd, _, _ = position()
+    keep_cross, keep_west, keep_east = inside()
     sea, u, v = [[spread(fields_ref[2 * k + r : 2 * k + r + 1, :]) for r in range(2)] for k in range(3)]
     lane = lane_ids()
     odd_lane = lax.rem(lane, 2) == 1
@@ -315,9 +323,9 @@
         border = []
         for r in range(2):
             rows = side_rows(group, r)
-            border.append(
-                jnp.where(odd_lane, west_in[rows, :], pltpu.roll(east_in[rows, :], LANES - 2, 1))
-            )
+            from_west = keep_west * west_in[rows, :]
+            from_east = pltpu.roll(keep_east * east_in[rows, :], LANES - 2, 1)
+            border.append(jnp.where(odd_lane, from_west, from_east))
 
         def turned(r, i):
             energy = e_ref[field_rows(group, r, i), :]
@@ -338,7 +346,7 @@
             energy = [here[r][0] for r in range(2)]
             py = [jnp.maximum(cy[r], 0.0) * energy[r] for r in range(2)]
             my = [jnp.minimum(cy[r], 0.0) * energy[r] for r in range(2)]
-            from_cross = fetch(cross_in, group, base, i)
+            from_cross = keep_cross * fetch(cross_in, group, base, i)
             from_chip = fetch(chip_in, group, base, mirrored(i))
             in_y = [from_cross - my[1], py[0] + from_chip]
             new = []
@@ -399,12 +407,14 @@
 
 def exchange(cross, chip, side):
     geo, spec = lax.axis_size("geo"), lax.axis_size("spec")
-    links = [(k, k + 1) for k in range(1, geo - 1, 2)]
+    place = lambda row, col: row * spec + col
+    links = [(place(k, c), place(k + 1, c)) for k in range(1, geo - 1, 2) for c in range(spec)]
+    links += [(place(k, c), place(k, c + 1)) for k in (0, geo - 1) for c in range(0, spec, 2)]
     cores = [(k, k + 1) for k in range(0, geo, 2)]
-    east = [(k, k + 1) for k in range(spec - 1)]
+    east = [(k, (k + 1) % spec) for k in range(spec)]
     both = lambda pairs: pairs + [(b, a) for a, b in pairs]
     return (
-        lax.ppermute(cross, "geo", both(links)),
+        lax.ppermute(cross, ("geo", "spec"), both(links)),
         lax.ppermute(chip, "geo", both(cores)),
         lax.ppermute(side, "spec", east),
         lax.ppermute(side, "spec", [(b, a) for a, b in east]),

time: 42.4 us -> 38.6 us (0.910)
  starting transfers between devices: 19.7 us -> 9.7 us
  waiting for transfers between devices: 12.1 us -> 18.5 us
    ppermute x2, starting transfers between devices: 9.1 us -> 0.01 us  [exchange(): lax.ppermute(side, 'spec', east)]
    ppermute x2, waiting for transfers between devices: 2.93 us -> 7.08 us  [exchange(): lax.ppermute(side, 'spec', east)]
    ppermute x2, starting transfers between devices: 7.81 us -> 4.17 us  [exchange(): lax.ppermute(cross, ('geo', 'spec'), both(links))]
    ppermute x2, waiting for transfers between devices: 0.69 us -> 3.69 us  [exchange(): lax.ppermute(side, 'spec', [(b, a) for a, b in east])]
    ppermute x2, starting transfers between devices: 2.58 us -> 5.52 us  [exchange(): lax.ppermute(side, 'spec', [(b, a) for a, b in east])]
    ppermute x2, waiting for transfers between devices: 8.49 us -> 7.77 us  [exchange(): lax.ppermute(cross, ('geo', 'spec'), both(links))]
where the time goes in v2:
time: 38.6 us; the launch traced here: 38.5 us
  waiting for transfers between devices  18.5 us (48%)
  Pallas kernels  10.2 us (26%)
  starting transfers between devices  9.7 us (25%)
    ppermute x2, waiting for transfers between devices, exchange(): lax.ppermute(cross, ('geo', 'spec'), both(links))  7.77 us
    ppermute x2, waiting for transfers between devices, exchange(): lax.ppermute(side, 'spec', east)  7.08 us
    ppermute x2, starting transfers between devices, exchange(): lax.ppermute(side, 'spec', [(b, a) for a, b in east])  5.52 us
    ppermute x2, starting transfers between devices, exchange(): lax.ppermute(cross, ('geo', 'spec'), both(links))  4.17 us
    ppermute x2, waiting for transfers between devices, exchange(): lax.ppermute(side, 'spec', [(b, a) for a, b in east])  3.69 us
    pallas_call x1, Pallas kernels, per_device(): pl.pallas_call(source_kernel, out_shape=packets() + [shape(FIELDS)], in_s...  3.6 us
    pallas_call x1, Pallas kernels, per_device(): pl.pallas_call(functools.partial(transport_kernel, True), out_shape=shape...  3.37 us
    pallas_call x1, Pallas kernels, per_device(): pl.pallas_call(functools.partial(transport_kernel, False), out_shape=pack...  3.29 us
  transfers between devices with their start and end apart: 8, of which 6 were waited for; matrix products, arithmetic and copies ran while one was open for 0% of the time, Pallas kernels for 0%

profile of v2, /device:TPU:128, one launch (start us, length us, event | category | flops | bytes accessed | tf_op | source)
XLA Modules:
  0.0 38.5 jit_solution(5632604412931453785)
XLA Ops:
  0.0 3.6 %source.1 = (f32[4032,128]{1,0:T(8,128)S(1)}, f32[1408,128]{1,0:T(8,128)S(1)}, f32[1408,128]{1,0:T(8,128)S(1)}, f32[112,128]{1,0:T(8,128)S(1)}, f32[80,128]{1,0:T(8,128)S(1)}) custom-call(f32[3600,128]{1,0:T(8,128)} %bitcast.2, f32[2,128]{1,0:T(2,128)} %refs_1_.1, f32[2,128]{1,0:T(2,128)} %refs_2_.1, f32[2,512]{1,0:T(2,128)} %refs_3_.1, f32[2,512]{1,0:T(2,128)} %refs_4_.1, ...), custom_call_target="tpu_custom_call" | custom-call | tf_op jit(solution)/shard_map/source/pallas_call | solution.py:431
  3.6 2.1 %collective-permute-start = (f32[1408,128]{1,0:T(8,128)S(1)}, f32[1408,128]{1,0:T(8,128)S(1)}, u32[]{:S(2)}, u32[]{:S(2)}) collective-permute-start(f32[1408,128]{1,0:T(8,128)S(1)} %get-tuple-element.15), channel_id=1, source_target_pairs={{4,8},{5,9},{6,10},{7,11},{12,16},{13,17},{14,18},{15,19},{20,24},... | collective-permute-start | bytes 2162696 | tf_op jit(solution)/shard_map/ppermute | solution.py:417
  5.7 0.0 collective-permute-start.1
  5.7 2.8 %collective-permute-start.3 = (f32[112,128]{1,0:T(8,128)S(1)}, f32[112,128]{1,0:T(8,128)S(1)}, u32[]{:S(2)}, u32[]{:S(2)}) collective-permute-start(f32[112,128]{1,0:T(8,128)S(1)} %get-tuple-element.17), channel_id=1, source_target_pairs={{1,0},{2,1},{3,2},{0,3},{5,4},{6,5},{7,6},{4,7},{9,8},{10,9},{11,1... | collective-permute-start | bytes 172040 | tf_op jit(solution)/shard_map/ppermute | solution.py:420
  8.5 0.0 collective-permute-start.2
  8.5 1.8 %collective-permute-done.3.east_in = f32[112,128]{1,0:T(8,128)S(1)} collective-permute-done((f32[112,128]{1,0:T(8,128)S(1)}, f32[112,128]{1,0:T(8,128)S(1)}, u32[]{:S(2)}, u32[]{:S(2)}) %collective-permute-start.3) | collective-permute-done | bytes 57376 | tf_op jit(solution)/shard_map/ppermute | solution.py:420
  10.3 3.5 %collective-permute-done.2.west_in = f32[112,128]{1,0:T(8,128)S(1)} collective-permute-done((f32[112,128]{1,0:T(8,128)S(1)}, f32[112,128]{1,0:T(8,128)S(1)}, u32[]{:S(2)}, u32[]{:S(2)}) %collective-permute-start.2) | collective-permute-done | bytes 57376 | tf_op jit(solution)/shard_map/ppermute | solution.py:419
  13.8 3.9 %collective-permute-done.cross_in = f32[1408,128]{1,0:T(8,128)S(1)} collective-permute-done((f32[1408,128]{1,0:T(8,128)S(1)}, f32[1408,128]{1,0:T(8,128)S(1)}, u32[]{:S(2)}, u32[]{:S(2)}) %collective-permute-start) | collective-permute-done | bytes 720928 | tf_op jit(solution)/shard_map/ppermute | solution.py:417
  17.7 0.0 collective-permute-done.1.chip_in
  17.7 3.3 %first_substep.1 = (f32[4032,128]{1,0:T(8,128)S(1)}, f32[1408,128]{1,0:T(8,128)S(1)}, f32[1408,128]{1,0:T(8,128)S(1)}, f32[112,128]{1,0:T(8,128)S(1)}) custom-call(f32[4032,128]{1,0:T(8,128)S(1)} %get-tuple-element.14.e_ref, f32[1408,128]{1,0:T(8,128)S(1)} %collective-permute-done.cross_in, f32[1408,128]{1,0:T(8,128)S(1)} %collective-permute-done.1.chip_in, ...), custom_call_target="tpu_custom_call" | custom-call | tf_op jit(solution)/shard_map/first_substep/pallas_call | solution.py:443
  21.0 2.1 %collective-permute-start.4 = (f32[1408,128]{1,0:T(8,128)S(1)}, f32[1408,128]{1,0:T(8,128)S(1)}, u32[]{:S(2)}, u32[]{:S(2)}) collective-permute-start(f32[1408,128]{1,0:T(8,128)S(1)} %get-tuple-element.20), channel_id=1, source_target_pairs={{4,8},{5,9},{6,10},{7,11},{12,16},{13,17},{14,18},{15,19},{20,24},... | collective-permute-start | bytes 2162696 | tf_op jit(solution)/shard_map/ppermute | solution.py:417
  23.1 0.0 collective-permute-start.5
  23.1 2.8 %collective-permute-start.7 = (f32[112,128]{1,0:T(8,128)S(1)}, f32[112,128]{1,0:T(8,128)S(1)}, u32[]{:S(2)}, u32[]{:S(2)}) collective-permute-start(f32[112,128]{1,0:T(8,128)S(1)} %get-tuple-element.22), channel_id=1, source_target_pairs={{1,0},{2,1},{3,2},{0,3},{5,4},{6,5},{7,6},{4,7},{9,8},{10,9},{11,1... | collective-permute-start | bytes 172040 | tf_op jit(solution)/shard_map/ppermute | solution.py:420
  25.9 0.0 collective-permute-start.6
  25.9 1.8 %collective-permute-done.7.east_in = f32[112,128]{1,0:T(8,128)S(1)} collective-permute-done((f32[112,128]{1,0:T(8,128)S(1)}, f32[112,128]{1,0:T(8,128)S(1)}, u32[]{:S(2)}, u32[]{:S(2)}) %collective-permute-start.7) | collective-permute-done | bytes 57376 | tf_op jit(solution)/shard_map/ppermute | solution.py:420
  27.7 3.5 %collective-permute-done.6.west_in = f32[112,128]{1,0:T(8,128)S(1)} collective-permute-done((f32[112,128]{1,0:T(8,128)S(1)}, f32[112,128]{1,0:T(8,128)S(1)}, u32[]{:S(2)}, u32[]{:S(2)}) %collective-permute-start.6) | collective-permute-done | bytes 57376 | tf_op jit(solution)/shard_map/ppermute | solution.py:419
  31.3 3.9 %collective-permute-done.4.cross_in = f32[1408,128]{1,0:T(8,128)S(1)} collective-permute-done((f32[1408,128]{1,0:T(8,128)S(1)}, f32[1408,128]{1,0:T(8,128)S(1)}, u32[]{:S(2)}, u32[]{:S(2)}) %collective-permute-start.4) | collective-permute-done | bytes 720928 | tf_op jit(solution)/shard_map/ppermute | solution.py:417
  35.1 0.0 collective-permute-done.5.chip_in
  35.1 3.4 %second_substep.1 = f32[3600,128]{1,0:T(8,128)} custom-call(f32[4032,128]{1,0:T(8,128)S(1)} %get-tuple-element.19.e_ref, f32[1408,128]{1,0:T(8,128)S(1)} %collective-permute-done.4.cross_in, f32[1408,128]{1,0:T(8,128)S(1)} %collective-permute-done.5.chip_in, f32[112,128]{1,0:T(8,128)S(1)} %collective-permute-done.6.west_in, ...), custom_call_target="tpu_custom_call" | custom-call | tf_op jit(solution)/shard_map/second_substep/pallas_call | solution.py:452
Async XLA Ops:
  3.6 14.1 %collective-permute-start = (f32[1408,128]{1,0:T(8,128)S(1)}, f32[1408,128]{1,0:T(8,128)S(1)}, u32[]{:S(2)}, u32[]{:S(2)}) collective-permute-start(f32[1408,128]{1,0:T(8,128)S(1)} %get-tuple-element.15), channel_id=1, source_target_pairs={{4,8},{5,9},{6,10},{7,11},{12,16},{13,17},{14,18},{15,19},{20,24},... | collective-permute-start | bytes 2162696 | tf_op jit(solution)/shard_map/ppermute | solution.py:417
  5.7 12.0 %collective-permute-start.1 = (f32[1408,128]{1,0:T(8,128)S(1)}, f32[1408,128]{1,0:T(8,128)S(1)}, u32[]{:S(2)}, u32[]{:S(2)}) collective-permute-start(f32[1408,128]{1,0:T(8,128)S(1)} %get-tuple-element.16), channel_id=1, source_target_pairs={{0,4},{8,12},{16,20},{24,28},{32,36},{40,44},{48,52},{56,60},{64,6... | collective-permute-start | bytes 2162696 | tf_op jit(solution)/shard_map/ppermute | solution.py:418
  5.7 4.6 %collective-permute-start.3 = (f32[112,128]{1,0:T(8,128)S(1)}, f32[112,128]{1,0:T(8,128)S(1)}, u32[]{:S(2)}, u32[]{:S(2)}) collective-permute-start(f32[112,128]{1,0:T(8,128)S(1)} %get-tuple-element.17), channel_id=1, source_target_pairs={{1,0},{2,1},{3,2},{0,3},{5,4},{6,5},{7,6},{4,7},{9,8},{10,9},{11,1... | collective-permute-start | bytes 172040 | tf_op jit(solution)/shard_map/ppermute | solution.py:420
  8.5 5.4 %collective-permute-start.2 = (f32[112,128]{1,0:T(8,128)S(1)}, f32[112,128]{1,0:T(8,128)S(1)}, u32[]{:S(2)}, u32[]{:S(2)}) collective-permute-start(f32[112,128]{1,0:T(8,128)S(1)} %get-tuple-element.17), channel_id=1, source_target_pairs={{0,1},{1,2},{2,3},{3,0},{4,5},{5,6},{6,7},{7,4},{8,9},{9,10},{10,1... | collective-permute-start | bytes 172040 | tf_op jit(solution)/shard_map/ppermute | solution.py:419
  21.0 14.1 %collective-permute-start.4 = (f32[1408,128]{1,0:T(8,128)S(1)}, f32[1408,128]{1,0:T(8,128)S(1)}, u32[]{:S(2)}, u32[]{:S(2)}) collective-permute-start(f32[1408,128]{1,0:T(8,128)S(1)} %get-tuple-element.20), channel_id=1, source_target_pairs={{4,8},{5,9},{6,10},{7,11},{12,16},{13,17},{14,18},{15,19},{20,24},... | collective-permute-start | bytes 2162696 | tf_op jit(solution)/shard_map/ppermute | solution.py:417
  23.1 12.0 %collective-permute-start.5 = (f32[1408,128]{1,0:T(8,128)S(1)}, f32[1408,128]{1,0:T(8,128)S(1)}, u32[]{:S(2)}, u32[]{:S(2)}) collective-permute-start(f32[1408,128]{1,0:T(8,128)S(1)} %get-tuple-element.21), channel_id=1, source_target_pairs={{0,4},{8,12},{16,20},{24,28},{32,36},{40,44},{48,52},{56,60},{64,6... | collective-permute-start | bytes 2162696 | tf_op jit(solution)/shard_map/ppermute | solution.py:418
  23.1 4.6 %collective-permute-start.7 = (f32[112,128]{1,0:T(8,128)S(1)}, f32[112,128]{1,0:T(8,128)S(1)}, u32[]{:S(2)}, u32[]{:S(2)}) collective-permute-start(f32[112,128]{1,0:T(8,128)S(1)} %get-tuple-element.22), channel_id=1, source_target_pairs={{1,0},{2,1},{3,2},{0,3},{5,4},{6,5},{7,6},{4,7},{9,8},{10,9},{11,1... | collective-permute-start | bytes 172040 | tf_op jit(solution)/shard_map/ppermute | solution.py:420
  25.9 5.4 %collective-permute-start.6 = (f32[112,128]{1,0:T(8,128)S(1)}, f32[112,128]{1,0:T(8,128)S(1)}, u32[]{:S(2)}, u32[]{:S(2)}) collective-permute-start(f32[112,128]{1,0:T(8,128)S(1)} %get-tuple-element.22), channel_id=1, source_target_pairs={{0,1},{1,2},{2,3},{3,0},{4,5},{5,6},{6,7},{7,4},{8,9},{9,10},{10,1... | collective-permute-start | bytes 172040 | tf_op jit(solution)/shard_map/ppermute | solution.py:419

commit v3 on v2

--- a/solution.py
+++ b/solution.py
@@ -45,6 +45,7 @@
 TURN = 8
 FIELDS = TURN + 2 * ND
 BATCH = 3
+SPAN = 2 * 10**10
 CHUNK = SUB * 2 * ND
 FIELD = 2 * ND * PADF
 SIDE = 2 * PADF
@@ -169,10 +170,12 @@
             side_ref[side_rows(group, r), :] = self.total[r]
 
 
-def emit(i, energy, cx, cy, gather, cross, chip):
-    gather.put(i, energy, cx)
-    stores = cross.put(mirrored(i), jnp.maximum(-cy[0], 0.0) * energy[0])
-    return stores + chip.put(i, jnp.maximum(cy[1], 0.0) * energy[1])
+def cross_flux(cy, energy):
+    return jnp.maximum(-cy, 0.0) * energy
+
+
+def chip_flux(cy, energy):
+    return jnp.maximum(cy, 0.0) * energy
 
 
 def flush(stores):
@@ -186,16 +189,18 @@
     body(LAST)
 
 
-def finish_packets(cross_ref, chip_ref):
-    blank = jnp.zeros((SUB, LANES), F32)
-    cross_ref[SPARE:PACKET, :] = blank
-    chip_ref[SPARE:PACKET, :] = blank
+def finish_packet(ref):
+    ref[SPARE:PACKET, :] = jnp.zeros((SUB, LANES), F32)
+
+
+def field_of(fields_ref, kind):
+    return [spread(fields_ref[2 * kind + r : 2 * kind + r + 1, :]) for r in range(2)]
 
 
 def source_kernel(*refs):
     inputs, refs = refs[:8], refs[8:]
-    e_ref, cross_ref, chip_ref, side_ref, fields_ref, raw = refs[:6]
-    held, sems = refs[6:13], refs[13]
+    e_ref, cross_ref, side_ref, fields_ref, raw = refs[:5]
+    held, sems = refs[5:12], refs[12]
     odd, col, sign = position()
     copies = [
         pltpu.make_async_copy(source, target, sems.at[GROUPS + k])
@@ -245,7 +250,7 @@
     sums = stats(LAST, lax.fori_loop(0, LAST, stats, ((blank, blank), (blank, blank))))
     for copy in copies:
         copy.wait()
-    wind_x, wind_y, sea, decay, u, v = [], [], [], [], [], []
+    wind_x, wind_y, sea, decay, u = [], [], [], [], []
     for r in range(2):
         total = jnp.sum(sums[r][0], axis=0, keepdims=True)
         inverse = jnp.sum(sums[r][1], axis=0, keepdims=True)
@@ -266,7 +271,8 @@
             fields_ref[2 * k + r : 2 * k + r + 1, :] = own[k]
         sea.append(spread(own[0]))
         u.append(spread(own[1]))
-        v.append(spread(own[2]))
+        if r == 0:
+            v = spread(own[2])
         rx = row_of(rx_ref, odd, r, col)
         ry = sign * row_of(ry_ref, odd, r, col)
         for i in range(ND):
@@ -280,10 +286,10 @@
         gain = s * (source_seconds * wind_coef)
         damp = [sea[r] / (1.0 + decay[r] * s * s) for r in range(2)]
         base = group_base(group)
-        cross, chip = Sender(cross_ref, group, base), Sender(chip_ref, group, base)
+        cross = Sender(cross_ref, group, base)
         gather, stores = Gather(lane), []
         for i in range(ND):
-            energy, cx, cy = [], [], []
+            energy, cx = [], []
             for r in range(2):
                 rows = field_rows(group, r, i)
                 align = wind_x[r] * COS[i] + wind_y[r] * SIN[i]
@@ -292,40 +298,54 @@
                 stores.append((e_ref, rows, new))
                 energy.append(new)
                 cx.append(fc * COS[i] + u[r])
-                cy.append(fc * SIN[i] + v[r])
-            stores += emit(i, energy, cx, cy, gather, cross, chip)
+            gather.put(i, energy, cx)
+            stores += cross.put(mirrored(i), cross_flux(fc * SIN[i] + v, energy[0]))
             if i % BATCH == BATCH - 1:
                 flush(stores)
         gather.finish(side_ref, group)
 
     each_group(source)
-    finish_packets(cross_ref, chip_ref)
-
-
-def transport_kernel(last, e_ref, cross_in, chip_in, west_in, east_in, fields_ref, *rest):
-    if last:
-        out_hbm, work, sems = rest
+    finish_packet(cross_ref)
+
+
+def borders(group, sides, keep_west, keep_east, sign):
+    odd_lane = lax.rem(lane_ids(), 2) == 1
+    even_col = lax.rem(lax.axis_index("spec"), 2) == 0
+    out = []
+    for r in range(2):
+        first, second = [ref[side_rows(group, r), :] for ref in sides]
+        from_west = keep_west * jnp.where(even_col, second, first)
+        from_east = (sign * keep_east) * jnp.where(even_col, first, second)
+        from_east = pltpu.roll(from_east, LANES - 2, 1)
+        out.append(jnp.where(odd_lane, from_west, from_east))
+    return out
+
+
+def brought(border, i):
+    return pltpu.roll(border, (LANES - (2 * i + 1)) % LANES, 1)
+
+
+def speeds(group):
+    s, _ = radian_of(group)
+    c = (gravity / 2.0) / s
+    return courant_cells * c, (substep_seconds / DTH) * c
+
+
+def transport_kernel(first_step, *refs):
+    if first_step:
+        e_ref, *sides, fields_ref, out_ref, cross_ref, chip_ref = refs
     else:
-        out_ref, cross_ref, chip_ref, side_ref = rest
-    odd, _, _ = position()
-    keep_cross, keep_west, keep_east = inside()
-    sea, u, v = [[spread(fields_ref[2 * k + r : 2 * k + r + 1, :]) for r in range(2)] for k in range(3)]
+        e_ref, fields_ref, out_ref = refs
+    _, keep_west, keep_east = inside()
+    sea, u, v = [field_of(fields_ref, kind) for kind in range(3)]
     lane = lane_ids()
-    odd_lane = lax.rem(lane, 2) == 1
-    blank = jnp.zeros((SUB, LANES), F32)
 
     def substep(group):
-        s, _ = radian_of(group)
-        c = (gravity / 2.0) / s
-        fc = courant_cells * c
-        tc = (substep_seconds / DTH) * c
-        base = group_base(group)
-        border = []
-        for r in range(2):
-            rows = side_rows(group, r)
-            from_west = keep_west * west_in[rows, :]
-            from_east = pltpu.roll(keep_east * east_in[rows, :], LANES - 2, 1)
-            border.append(jnp.where(odd_lane, from_west, from_east))
+        fc, tc = speeds(group)
+        if first_step:
+            base = group_base(group)
+            border = borders(group, sides, keep_west, keep_east, 1.0)
+            cross, chip = Sender(cross_ref, group, base), Sender(chip_ref, group, base)
 
         def turned(r, i):
             energy = e_ref[field_rows(group, r, i), :]
@@ -336,9 +356,7 @@
         before = [turned(r, ND - 1)[1] for r in range(2)]
         first = [turned(r, 0) for r in range(2)]
         here = first
-        gather, stores = Gather(lane), []
-        if not last:
-            cross, chip = Sender(cross_ref, group, base), Sender(chip_ref, group, base)
+        stores = []
         for i in range(ND):
             after = [turned(r, i + 1) for r in range(2)] if i + 1 < ND else first
             cx = [fc * COS[i] + u[r] for r in range(2)]
@@ -346,50 +364,108 @@
             energy = [here[r][0] for r in range(2)]
             py = [jnp.maximum(cy[r], 0.0) * energy[r] for r in range(2)]
             my = [jnp.minimum(cy[r], 0.0) * energy[r] for r in range(2)]
-            from_cross = keep_cross * fetch(cross_in, group, base, i)
-            from_chip = fetch(chip_in, group, base, mirrored(i))
-            in_y = [from_cross - my[1], py[0] + from_chip]
+            in_y = [-my[1], py[0]]
             new = []
             for r in range(2):
                 px = jnp.maximum(cx[r], 0.0) * energy[r]
                 mx = jnp.minimum(cx[r], 0.0) * energy[r]
-                brought = pltpu.roll(border[r], (LANES - (2 * i + 1)) % LANES, 1)
-                px_in = jnp.where(lane == 0, brought, pltpu.roll(px, 1, 1))
-                mx_in = jnp.where(lane == LANES - 1, brought, pltpu.roll(mx, LANES - 1, 1))
+                edge = brought(border[r], i) if first_step else 0.0
+                px_in = jnp.where(lane == 0, edge, pltpu.roll(px, 1, 1))
+                mx_in = jnp.where(lane == LANES - 1, edge, pltpu.roll(mx, LANES - 1, 1))
                 stay = energy[r] - (px - mx) - (py[r] - my[r]) - (here[r][1] - here[r][2])
                 gained = (px_in - mx_in) + in_y[r] + (before[r] - after[r][2])
                 new.append(sea[r] * (stay + gained))
             for r in range(2):
-                if last:
-                    i_to = jnp.where(odd == 1, 2 * mirrored(i), 2 * i)
-                    r_to = jnp.where(odd == 1, 1 - r, r)
-                    start = group * CHUNK + i_to + r_to
-                    stores.append((work, pl.ds(start, SUB, stride=2 * ND), new[r]))
-                else:
-                    stores.append((out_ref, field_rows(group, r, i), new[r]))
-            if not last:
-                stores += emit(i, new, cx, cy, gather, cross, chip)
+                stores.append((out_ref, field_rows(group, r, i), new[r]))
+            if first_step:
+                stores += cross.put(mirrored(i), cross_flux(cy[0], new[0]))
+                stores += chip.put(i, py[1])
             if i % BATCH == BATCH - 1:
                 flush(stores)
             before = [here[r][1] for r in range(2)]
             here = after
-        if not last:
-            gather.finish(side_ref, group)
-
-        if last:
-            chunk(group).start()
+
+    each_group(substep)
+    if first_step:
+        finish_packet(cross_ref)
+        finish_packet(chip_ref)
+        cross_ref[PACKET:, :] = jnp.zeros((SUB, LANES), F32)
+        cross_ref[PACKET : PACKET + 1, :] = fields_ref[0:1, :]
+        cross_ref[PACKET + 1 : PACKET + 2, :] = fields_ref[4:5, :]
+
+
+def complete_kernel(part_ref, cross_in, chip_in, fields_ref, e_ref, chip_ref, side_ref):
+    keep_cross, _, _ = inside()
+    sea, u, v = [field_of(fields_ref, kind) for kind in range(3)]
+    sea_cross = keep_cross * sea[0]
+    lane = lane_ids()
+
+    def complete(group):
+        fc, _ = speeds(group)
+        base = group_base(group)
+        chip, gather, stores = Sender(chip_ref, group, base), Gather(lane), []
+        for i in range(ND):
+            rows = [field_rows(group, r, i) for r in range(2)]
+            new = [
+                part_ref[rows[0], :] + sea_cross * fetch(cross_in, group, base, i),
+                part_ref[rows[1], :] + sea[1] * fetch(chip_in, group, base, mirrored(i)),
+            ]
+            gather.put(i, new, [fc * COS[i] + u[r] for r in range(2)])
+            for r in range(2):
+                stores.append((e_ref, rows[r], new[r]))
+            stores += chip.put(i, chip_flux(fc * SIN[i] + v[1], new[1]))
+            if i % BATCH == BATCH - 1:
+                flush(stores)
+        gather.finish(side_ref, group)
+
+    each_group(complete)
+    finish_packet(chip_ref)
+
+
+def finish_kernel(
+    part_ref, sent_ref, cross_in, chip_in, side_a, side_b, fields_ref, out_hbm, work, sems
+):
+    odd, _, _ = position()
+    keep_cross, keep_west, keep_east = inside()
+    sea = field_of(fields_ref, 0)
+    sea_cross = keep_cross * sea[0]
+    their_sea = spread(cross_in[PACKET : PACKET + 1, :])
+    their_v = spread(cross_in[PACKET + 1 : PACKET + 2, :])
+    lane = lane_ids()
+    rim = jnp.where((lane == 0) | (lane == LANES - 1), 1.0, 0.0)
+    sea_rim = [sea[r] * rim for r in range(2)]
 
     def chunk(group):
         rows = pl.ds(group * CHUNK, TAIL * 2 * ND if group is LAST else CHUNK)
         return pltpu.make_async_copy(work.at[rows], out_hbm.at[rows], sems.at[group])
 
-    each_group(substep)
-    if last:
-        for group in range(LAST):
-            chunk(group).wait()
-        chunk(LAST).wait()
-    else:
-        finish_packets(cross_ref, chip_ref)
+    def finish(group):
+        fc, _ = speeds(group)
+        base = group_base(group)
+        border = borders(group, (side_a, side_b), keep_west, keep_east, -1.0)
+        stores = []
+        for i in range(ND):
+            passed = jnp.maximum(fc * SIN[i] - their_v, 0.0) * their_sea
+            back = fetch(sent_ref, group, base, mirrored(i))
+            from_cross = fetch(cross_in, group, base, i) + passed * back
+            from_rows = [
+                sea_cross * from_cross,
+                sea[1] * fetch(chip_in, group, base, mirrored(i)),
+            ]
+            for r in range(2):
+                from_cols = sea_rim[r] * brought(border[r], i)
+                new = part_ref[field_rows(group, r, i), :] + from_rows[r] + from_cols
+                i_to = jnp.where(odd == 1, 2 * mirrored(i), 2 * i)
+                r_to = jnp.where(odd == 1, 1 - r, r)
+                stores.append((work, pl.ds(group * CHUNK + i_to + r_to, SUB, stride=2 * ND), new))
+            if i % BATCH == BATCH - 1:
+                flush(stores)
+        chunk(group).start()
+
+    each_group(finish)
+    for group in range(LAST):
+        chunk(group).wait()
+    chunk(LAST).wait()
 
 
 VMEM = pl.BlockSpec(memory_space=pltpu.VMEM)
@@ -401,24 +477,42 @@
     return jax.ShapeDtypeStruct((rows, LANES), F32)
 
 
-def packets():
-    return [shape(FIELD), shape(PACKET), shape(PACKET), shape(SIDE)]
-
-
-def exchange(cross, chip, side):
+def call(kernel, outs, name, *args, span=0):
+    return pl.pallas_call(
+        kernel,
+        out_shape=[shape(rows) for rows in outs],
+        in_specs=[VMEM] * len(args),
+        out_specs=[VMEM] * len(outs),
+        compiler_params=PARAMS,
+        cost_estimate=pl.CostEstimate(flops=span, transcendentals=0, bytes_accessed=0),
+        name=name,
+    )(*args)
+
+
+def both(pairs):
+    return pairs + [(b, a) for a, b in pairs]
+
+
+def swap_cross(packet):
     geo, spec = lax.axis_size("geo"), lax.axis_size("spec")
     place = lambda row, col: row * spec + col
     links = [(place(k, c), place(k + 1, c)) for k in range(1, geo - 1, 2) for c in range(spec)]
     links += [(place(k, c), place(k, c + 1)) for k in (0, geo - 1) for c in range(0, spec, 2)]
-    cores = [(k, k + 1) for k in range(0, geo, 2)]
-    east = [(k, (k + 1) % spec) for k in range(spec)]
-    both = lambda pairs: pairs + [(b, a) for a, b in pairs]
-    return (
-        lax.ppermute(cross, ("geo", "spec"), both(links)),
-        lax.ppermute(chip, "geo", both(cores)),
-        lax.ppermute(side, "spec", east),
-        lax.ppermute(side, "spec", [(b, a) for a, b in east]),
-    )
+    return lax.ppermute(packet, ("geo", "spec"), both(links))
+
+
+def swap_chip(packet):
+    cores = [(k, k + 1) for k in range(0, lax.axis_size("geo"), 2)]
+    return lax.ppermute(packet, "geo", both(cores))
+
+
+def swap_columns(side):
+    geo, spec = lax.axis_size("geo"), lax.axis_size("spec")
+    place = lambda row, col: row * spec + col
+    inner = [(place(k, c), place(k, c + 1)) for k in range(geo) for c in range(0, spec, 2)]
+    outer = [(place(k, c), place(k, c + 1)) for k in range(geo) for c in range(1, spec - 1, 2)]
+    outer += [(place(k, c), place(k + 1, c)) for k in range(0, geo, 2) for c in (0, spec - 1)]
+    return [lax.ppermute(side, ("geo", "spec"), both(pairs)) for pairs in (inner, outer)]
 
 
 def per_device(
@@ -428,39 +522,50 @@
     flat = spectrum.reshape(rows, LANES)
     inputs = [flat, wind_speed, wind_dir, current_u, current_v, refract_x, refract_y, land_mask]
     inputs = [pltpu.with_memory_space_constraint(value, pltpu.HBM) for value in inputs]
-    energy, cross, chip, side, fields = pl.pallas_call(
+    energy, cross, side, fields = pl.pallas_call(
         source_kernel,
-        out_shape=packets() + [shape(FIELDS)],
+        out_shape=[shape(n) for n in (FIELD, PACKET, SIDE, FIELDS)],
         in_specs=[HBM] * len(inputs),
-        out_specs=[VMEM] * 5,
+        out_specs=[VMEM] * 4,
         scratch_shapes=[pltpu.VMEM((PADF * 2 * ND, LANES), F32)]
         + [pltpu.VMEM(value.shape, value.dtype) for value in inputs[1:]]
         + [pltpu.SemaphoreType.DMA((GROUPS + len(inputs) - 1,))],
         compiler_params=PARAMS,
         name="source",
     )(*inputs)
-    halo = exchange(cross, chip, side)
-    energy, cross, chip, side = pl.pallas_call(
-        functools.partial(transport_kernel, False),
-        out_shape=packets(),
-        in_specs=[VMEM] * 6,
-        out_specs=[VMEM] * 4,
-        compiler_params=PARAMS,
-        name="first_substep",
-    )(energy, *halo, fields)
-    halo = exchange(cross, chip, side)
+    sides = swap_columns(side)
+    cross_in = swap_cross(cross)
+    part, late, chip = call(
+        functools.partial(transport_kernel, True),
+        (FIELD, PACKET + SUB, PACKET),
+        "first_substep",
+        energy,
+        *sides,
+        fields,
+        span=SPAN,
+    )
+    late_in = swap_cross(late)
+    chip_in = swap_chip(chip)
+    energy, chip, side = call(
+        complete_kernel, (FIELD, PACKET, SIDE), "complete", part, cross_in, chip_in, fields
+    )
+    sides = swap_columns(side)
+    chip_in = swap_chip(chip)
+    (part,) = call(
+        functools.partial(transport_kernel, False), (FIELD,), "second_substep", energy, fields
+    )
     out = pl.pallas_call(
-        functools.partial(transport_kernel, True),
+        finish_kernel,
         out_shape=shape(rows),
-        in_specs=[VMEM] * 6,
+        in_specs=[VMEM] * 7,
         out_specs=HBM,
         scratch_shapes=[
             pltpu.VMEM((PADF * 2 * ND, LANES), F32),
             pltpu.SemaphoreType.DMA((GROUPS,)),
         ],
         compiler_params=PARAMS,
-        name="second_substep",
-    )(energy, *halo, fields)
+        name="finish",
+    )(part, cross, late_in, chip_in, *sides, fields)
     return out.reshape(spectrum.shape)
 
 

time: 38.6 us -> 30.9 us (0.80)
  waiting for transfers between devices: 18.5 us -> 9.73 us
  Pallas kernels: 10.2 us -> 11.9 us
  starting transfers between devices: 9.7 us -> 9.08 us
    ppermute x8, waiting for transfers between devices: 18.5 us -> 9.73 us  [the longest x2 9 us: swap_cross(): return lax.ppermute(packet, ('geo', 'spec'), both(links))]
    pallas_call x3 -> x5, Pallas kernels: 10.2 us -> 11.9 us  [the longest x3 6.03 us: call(): pl.pallas_call(kernel, out_shape=[shape(rows) for rows in outs], in_specs...]
    ppermute x8, starting transfers between devices: 9.7 us -> 9.08 us  [the longest x4 4.45 us: swap_columns(): lax.ppermute(side, ('geo', 'spec'), both(pairs))]
  transfers between devices with their start and end apart: 8 -> 8, of which waited for: 6 -> 3; matrix products, arithmetic and copies ran while one was open for 0% -> 0% of each run, Pallas kernels for 0% -> 20%
where the time goes in v3:
time: 30.9 us; the launch traced here: 30.8 us
  Pallas kernels  11.9 us (39%)
  waiting for transfers between devices  9.73 us (31%)
  starting transfers between devices  9.08 us (29%)
    ppermute x2, waiting for transfers between devices, swap_cross(): return lax.ppermute(packet, ('geo', 'spec'), both(links))  9 us
    pallas_call x3, Pallas kernels, call(): pl.pallas_call(kernel, out_shape=[shape(rows) for rows in outs], in_specs...  6.03 us
    ppermute x4, starting transfers between devices, swap_columns(): lax.ppermute(side, ('geo', 'spec'), both(pairs))  4.45 us
    ppermute x2, starting transfers between devices, swap_cross(): return lax.ppermute(packet, ('geo', 'spec'), both(links))  4.44 us
    pallas_call x1, Pallas kernels, per_device(): pl.pallas_call(source_kernel, out_shape=[shape(n) for n in (FIELD, PACKET...  3.51 us
    pallas_call x1, Pallas kernels, per_device(): pl.pallas_call(finish_kernel, out_shape=shape(rows), in_specs=[VMEM] * 7,...  2.37 us
    ppermute x4, waiting for transfers between devices, swap_columns(): lax.ppermute(side, ('geo', 'spec'), both(pairs))  0.72 us
  transfers between devices with their start and end apart: 8, of which 3 were waited for; matrix products, arithmetic and copies ran while one was open for 0% of the time, Pallas kernels for 20%

profile of v3, /device:TPU:128, one launch (start us, length us, event | category | flops | bytes accessed | tf_op | source)
XLA Modules:
  0.0 30.8 jit_solution(12142945791286085386)
XLA Ops:
  0.0 3.5 %source.1 = (f32[4032,128]{1,0:T(8,128)S(1)}, f32[1408,128]{1,0:T(8,128)S(1)}, f32[112,128]{1,0:T(8,128)S(1)}, f32[80,128]{1,0:T(8,128)S(1)}) custom-call(f32[3600,128]{1,0:T(8,128)} %bitcast.2, f32[2,128]{1,0:T(2,128)} %refs_1_.1, f32[2,128]{1,0:T(2,128)} %refs_2_.1, f32[2,512]{1,0:T(2,128)} %refs_3_.1, f32[2,512]{1,0:T(2,128)} %refs_4_.1, ...), custom_call_target="tpu_custom_call" | custom-call | tf_op jit(solution)/shard_map/source/pallas_call | solution.py:525
  3.5 0.1 collective-permute-start.1
  3.6 3.0 %collective-permute-start = (f32[112,128]{1,0:T(8,128)S(1)}, f32[112,128]{1,0:T(8,128)S(1)}, u32[]{:S(2)}, u32[]{:S(2)}) collective-permute-start(f32[112,128]{1,0:T(8,128)S(1)} %get-tuple-element.16), channel_id=1, source_target_pairs={{0,1},{2,3},{4,5},{6,7},{8,9},{10,11},{12,13},{14,15},{16,17},{18,... | collective-permute-start | bytes 172040 | tf_op jit(solution)/shard_map/ppermute | solution.py:515
  6.6 1.4 %collective-permute-start.2 = (f32[1408,128]{1,0:T(8,128)S(1)}, f32[1408,128]{1,0:T(8,128)S(1)}, u32[]{:S(2)}, u32[]{:S(2)}) collective-permute-start(f32[1408,128]{1,0:T(8,128)S(1)} %get-tuple-element.19.sent_ref), channel_id=1, source_target_pairs={{4,8},{5,9},{6,10},{7,11},{12,16},{13,17},{14,18},{15,19},{20,24},... | collective-permute-start | bytes 2162696 | tf_op jit(solution)/shard_map/ppermute | solution.py:501
  8.0 0.0 collective-permute-done.1.refs_2_
  8.0 0.7 %collective-permute-done.refs_1_ = f32[112,128]{1,0:T(8,128)S(1)} collective-permute-done((f32[112,128]{1,0:T(8,128)S(1)}, f32[112,128]{1,0:T(8,128)S(1)}, u32[]{:S(2)}, u32[]{:S(2)}) %collective-permute-start) | collective-permute-done | bytes 57376 | tf_op jit(solution)/shard_map/ppermute | solution.py:515
  8.7 2.6 %first_substep.1 = (f32[4032,128]{1,0:T(8,128)S(1)}, f32[1416,128]{1,0:T(8,128)S(1)}, f32[1408,128]{1,0:T(8,128)S(1)}) custom-call(f32[4032,128]{1,0:T(8,128)S(1)} %get-tuple-element.15.refs_0_, f32[112,128]{1,0:T(8,128)S(1)} %collective-permute-done.refs_1_, f32[112,128]{1,0:T(8,128)S(1)} %collective-permute-done.1.refs_2_, ...), custom_call_target="tpu_custom_call" | custom-call | flops 20000000000 | tf_op jit(solution)/shard_map/first_substep/pallas_call | solution.py:481
  11.3 0.1 collective-permute-start.3
  11.4 3.0 %collective-permute-start.4 = (f32[1416,128]{1,0:T(8,128)S(1)}, f32[1416,128]{1,0:T(8,128)S(1)}, u32[]{:S(2)}, u32[]{:S(2)}) collective-permute-start(f32[1416,128]{1,0:T(8,128)S(1)} %get-tuple-element.22), channel_id=1, source_target_pairs={{4,8},{5,9},{6,10},{7,11},{12,16},{13,17},{14,18},{15,19},{20,24},... | collective-permute-start | bytes 2174984 | tf_op jit(solution)/shard_map/ppermute | solution.py:501
  14.4 6.2 %collective-permute-done.2.cross_in = f32[1408,128]{1,0:T(8,128)S(1)} collective-permute-done((f32[1408,128]{1,0:T(8,128)S(1)}, f32[1408,128]{1,0:T(8,128)S(1)}, u32[]{:S(2)}, u32[]{:S(2)}) %collective-permute-start.2) | collective-permute-done | bytes 720928 | tf_op jit(solution)/shard_map/ppermute | solution.py:501
  20.6 0.0 collective-permute-done.3.chip_in
  20.6 1.2 %complete.1 = (f32[4032,128]{1,0:T(8,128)S(1)}, f32[1408,128]{1,0:T(8,128)S(1)}, f32[112,128]{1,0:T(8,128)S(1)}) custom-call(f32[4032,128]{1,0:T(8,128)S(1)} %get-tuple-element.18.part_ref, f32[1408,128]{1,0:T(8,128)S(1)} %collective-permute-done.2.cross_in, f32[1408,128]{1,0:T(8,128)S(1)} %collective-permute-done.3.chip_in, ...), custom_call_target="tpu_custom_call" | custom-call | tf_op jit(solution)/shard_map/complete/pallas_call | solution.py:481
  21.9 0.1 collective-permute-start.5
  22.0 0.5 %collective-permute-start.7 = (f32[112,128]{1,0:T(8,128)S(1)}, f32[112,128]{1,0:T(8,128)S(1)}, u32[]{:S(2)}, u32[]{:S(2)}) collective-permute-start(f32[112,128]{1,0:T(8,128)S(1)} %get-tuple-element.24), channel_id=1, source_target_pairs={{1,2},{5,6},{9,10},{13,14},{17,18},{21,22},{25,26},{29,30},{33,34}... | collective-permute-start | bytes 172040 | tf_op jit(solution)/shard_map/ppermute | solution.py:515
  22.5 0.9 %collective-permute-start.6 = (f32[112,128]{1,0:T(8,128)S(1)}, f32[112,128]{1,0:T(8,128)S(1)}, u32[]{:S(2)}, u32[]{:S(2)}) collective-permute-start(f32[112,128]{1,0:T(8,128)S(1)} %get-tuple-element.24), channel_id=1, source_target_pairs={{0,1},{2,3},{4,5},{6,7},{8,9},{10,11},{12,13},{14,15},{16,17},{18,... | collective-permute-start | bytes 172040 | tf_op jit(solution)/shard_map/ppermute | solution.py:515
  23.3 2.2 %second_substep.1.part_ref = f32[4032,128]{1,0:T(8,128)S(1)} custom-call(f32[4032,128]{1,0:T(8,128)S(1)} %get-tuple-element.21.refs_0_, f32[80,128]{1,0:T(8,128)S(1)} %get-tuple-element.17.refs_3_.fields_ref.refs_1_), custom_call_target="tpu_custom_call" | custom-call | tf_op jit(solution)/shard_map/second_substep/pallas_call | solution.py:481
  25.6 2.8 %collective-permute-done.4.cross_in = f32[1416,128]{1,0:T(8,128)S(1)} collective-permute-done((f32[1416,128]{1,0:T(8,128)S(1)}, f32[1416,128]{1,0:T(8,128)S(1)}, u32[]{:S(2)}, u32[]{:S(2)}) %collective-permute-start.4) | collective-permute-done | bytes 725024 | tf_op jit(solution)/shard_map/ppermute | solution.py:501
  28.4 0.0 collective-permute-done.7.side_b
  28.4 0.0 collective-permute-done.6.side_a
  28.4 0.0 collective-permute-done.5.chip_in
  28.4 2.4 %finish.1 = f32[3600,128]{1,0:T(8,128)} custom-call(f32[4032,128]{1,0:T(8,128)S(1)} %second_substep.1.part_ref, f32[1408,128]{1,0:T(8,128)S(1)} %get-tuple-element.19.sent_ref, f32[1416,128]{1,0:T(8,128)S(1)} %collective-permute-done.4.cross_in, f32[1408,128]{1,0:T(8,128)S(1)} %collective-permute-done.5.chip_in, ...), custom_call_target="tpu_custom_call" | custom-call | tf_op jit(solution)/shard_map/finish/pallas_call | solution.py:557
Async XLA Ops:
  3.5 4.5 %collective-permute-start.1 = (f32[112,128]{1,0:T(8,128)S(1)}, f32[112,128]{1,0:T(8,128)S(1)}, u32[]{:S(2)}, u32[]{:S(2)}) collective-permute-start(f32[112,128]{1,0:T(8,128)S(1)} %get-tuple-element.16), channel_id=1, source_target_pairs={{1,2},{5,6},{9,10},{13,14},{17,18},{21,22},{25,26},{29,30},{33,34}... | collective-permute-start | bytes 172040 | tf_op jit(solution)/shard_map/ppermute | solution.py:515
  3.6 5.1 %collective-permute-start = (f32[112,128]{1,0:T(8,128)S(1)}, f32[112,128]{1,0:T(8,128)S(1)}, u32[]{:S(2)}, u32[]{:S(2)}) collective-permute-start(f32[112,128]{1,0:T(8,128)S(1)} %get-tuple-element.16), channel_id=1, source_target_pairs={{0,1},{2,3},{4,5},{6,7},{8,9},{10,11},{12,13},{14,15},{16,17},{18,... | collective-permute-start | bytes 172040 | tf_op jit(solution)/shard_map/ppermute | solution.py:515
  6.6 14.0 %collective-permute-start.2 = (f32[1408,128]{1,0:T(8,128)S(1)}, f32[1408,128]{1,0:T(8,128)S(1)}, u32[]{:S(2)}, u32[]{:S(2)}) collective-permute-start(f32[1408,128]{1,0:T(8,128)S(1)} %get-tuple-element.19.sent_ref), channel_id=1, source_target_pairs={{4,8},{5,9},{6,10},{7,11},{12,16},{13,17},{14,18},{15,19},{20,24},... | collective-permute-start | bytes 2162696 | tf_op jit(solution)/shard_map/ppermute | solution.py:501
  11.3 9.3 %collective-permute-start.3 = (f32[1408,128]{1,0:T(8,128)S(1)}, f32[1408,128]{1,0:T(8,128)S(1)}, u32[]{:S(2)}, u32[]{:S(2)}) collective-permute-start(f32[1408,128]{1,0:T(8,128)S(1)} %get-tuple-element.20), channel_id=1, source_target_pairs={{0,4},{8,12},{16,20},{24,28},{32,36},{40,44},{48,52},{56,60},{64,6... | collective-permute-start | bytes 2162696 | tf_op jit(solution)/shard_map/ppermute | solution.py:506
  11.4 17.0 %collective-permute-start.4 = (f32[1416,128]{1,0:T(8,128)S(1)}, f32[1416,128]{1,0:T(8,128)S(1)}, u32[]{:S(2)}, u32[]{:S(2)}) collective-permute-start(f32[1416,128]{1,0:T(8,128)S(1)} %get-tuple-element.22), channel_id=1, source_target_pairs={{4,8},{5,9},{6,10},{7,11},{12,16},{13,17},{14,18},{15,19},{20,24},... | collective-permute-start | bytes 2174984 | tf_op jit(solution)/shard_map/ppermute | solution.py:501
  21.9 6.5 %collective-permute-start.5 = (f32[1408,128]{1,0:T(8,128)S(1)}, f32[1408,128]{1,0:T(8,128)S(1)}, u32[]{:S(2)}, u32[]{:S(2)}) collective-permute-start(f32[1408,128]{1,0:T(8,128)S(1)} %get-tuple-element.23), channel_id=1, source_target_pairs={{0,4},{8,12},{16,20},{24,28},{32,36},{40,44},{48,52},{56,60},{64,6... | collective-permute-start | bytes 2162696 | tf_op jit(solution)/shard_map/ppermute | solution.py:506
  22.0 6.4 %collective-permute-start.7 = (f32[112,128]{1,0:T(8,128)S(1)}, f32[112,128]{1,0:T(8,128)S(1)}, u32[]{:S(2)}, u32[]{:S(2)}) collective-permute-start(f32[112,128]{1,0:T(8,128)S(1)} %get-tuple-element.24), channel_id=1, source_target_pairs={{1,2},{5,6},{9,10},{13,14},{17,18},{21,22},{25,26},{29,30},{33,34}... | collective-permute-start | bytes 172040 | tf_op jit(solution)/shard_map/ppermute | solution.py:515
  22.5 5.9 %collective-permute-start.6 = (f32[112,128]{1,0:T(8,128)S(1)}, f32[112,128]{1,0:T(8,128)S(1)}, u32[]{:S(2)}, u32[]{:S(2)}) collective-permute-start(f32[112,128]{1,0:T(8,128)S(1)} %get-tuple-element.24), channel_id=1, source_target_pairs={{0,1},{2,3},{4,5},{6,7},{8,9},{10,11},{12,13},{14,15},{16,17},{18,... | collective-permute-start | bytes 172040 | tf_op jit(solution)/shard_map/ppermute | solution.py:515

commit v4 on v3

--- a/solution.py
+++ b/solution.py
@@ -45,6 +45,7 @@
 TURN = 8
 FIELDS = TURN + 2 * ND
 BATCH = 3
+FAR_BATCH = 6
 SPAN = 2 * 10**10
 CHUNK = SUB * 2 * ND
 FIELD = 2 * ND * PADF
@@ -313,7 +314,7 @@
     even_col = lax.rem(lax.axis_index("spec"), 2) == 0
     out = []
     for r in range(2):
-        first, second = [ref[side_rows(group, r), :] for ref in sides]
+        second, first = [ref[side_rows(group, r), :] for ref in sides]
         from_west = keep_west * jnp.where(even_col, second, first)
         from_east = (sign * keep_east) * jnp.where(even_col, first, second)
         from_east = pltpu.roll(from_east, LANES - 2, 1)
@@ -422,47 +423,64 @@
     finish_packet(chip_ref)
 
 
-def finish_kernel(
-    part_ref, sent_ref, cross_in, chip_in, side_a, side_b, fields_ref, out_hbm, work, sems
-):
-    odd, _, _ = position()
-    keep_cross, keep_west, keep_east = inside()
+def places(group, r, i, odd):
+    i_to = jnp.where(odd == 1, 2 * mirrored(i), 2 * i)
+    r_to = jnp.where(odd == 1, 1 - r, r)
+    return pl.ds(group * CHUNK + i_to + r_to, SUB, stride=2 * ND)
+
+
+def near_kernel(part_ref, chip_in, side_a, side_b, fields_ref, out_ref):
+    _, keep_west, keep_east = inside()
     sea = field_of(fields_ref, 0)
-    sea_cross = keep_cross * sea[0]
-    their_sea = spread(cross_in[PACKET : PACKET + 1, :])
-    their_v = spread(cross_in[PACKET + 1 : PACKET + 2, :])
     lane = lane_ids()
     rim = jnp.where((lane == 0) | (lane == LANES - 1), 1.0, 0.0)
     sea_rim = [sea[r] * rim for r in range(2)]
 
+    def near(group):
+        base = group_base(group)
+        border = borders(group, (side_a, side_b), keep_west, keep_east, -1.0)
+        stores = []
+        for i in range(ND):
+            for r in range(2):
+                rows = field_rows(group, r, i)
+                new = part_ref[rows, :] + sea_rim[r] * brought(border[r], i)
+                if r == 1:
+                    new = new + sea[1] * fetch(chip_in, group, base, mirrored(i))
+                stores.append((out_ref, rows, new))
+            if i % BATCH == BATCH - 1:
+                flush(stores)
+
+    each_group(near)
+
+
+def far_kernel(part_ref, sent_ref, cross_in, fields_ref, out_hbm, work, sems):
+    odd, _, _ = position()
+    keep_cross, _, _ = inside()
+    sea_cross = keep_cross * field_of(fields_ref, 0)[0]
+    their_sea = spread(cross_in[PACKET : PACKET + 1, :])
+    their_v = spread(cross_in[PACKET + 1 : PACKET + 2, :])
+
     def chunk(group):
         rows = pl.ds(group * CHUNK, TAIL * 2 * ND if group is LAST else CHUNK)
         return pltpu.make_async_copy(work.at[rows], out_hbm.at[rows], sems.at[group])
 
-    def finish(group):
+    def far(group):
         fc, _ = speeds(group)
         base = group_base(group)
-        border = borders(group, (side_a, side_b), keep_west, keep_east, -1.0)
         stores = []
         for i in range(ND):
             passed = jnp.maximum(fc * SIN[i] - their_v, 0.0) * their_sea
             back = fetch(sent_ref, group, base, mirrored(i))
             from_cross = fetch(cross_in, group, base, i) + passed * back
-            from_rows = [
-                sea_cross * from_cross,
-                sea[1] * fetch(chip_in, group, base, mirrored(i)),
-            ]
+            new = [part_ref[field_rows(group, r, i), :] for r in range(2)]
+            new[0] = new[0] + sea_cross * from_cross
             for r in range(2):
-                from_cols = sea_rim[r] * brought(border[r], i)
-                new = part_ref[field_rows(group, r, i), :] + from_rows[r] + from_cols
-                i_to = jnp.where(odd == 1, 2 * mirrored(i), 2 * i)
-                r_to = jnp.where(odd == 1, 1 - r, r)
-                stores.append((work, pl.ds(group * CHUNK + i_to + r_to, SUB, stride=2 * ND), new))
-            if i % BATCH == BATCH - 1:
+                stores.append((work, places(group, r, i, odd), new[r]))
+            if i % FAR_BATCH == FAR_BATCH - 1:
                 flush(stores)
         chunk(group).start()
 
-    each_group(finish)
+    each_group(far)
     for group in range(LAST):
         chunk(group).wait()
     chunk(LAST).wait()
@@ -512,7 +530,7 @@
     inner = [(place(k, c), place(k, c + 1)) for k in range(geo) for c in range(0, spec, 2)]
     outer = [(place(k, c), place(k, c + 1)) for k in range(geo) for c in range(1, spec - 1, 2)]
     outer += [(place(k, c), place(k + 1, c)) for k in range(0, geo, 2) for c in (0, spec - 1)]
-    return [lax.ppermute(side, ("geo", "spec"), both(pairs)) for pairs in (inner, outer)]
+    return [lax.ppermute(side, ("geo", "spec"), both(pairs)) for pairs in (outer, inner)]
 
 
 def per_device(
@@ -554,18 +572,19 @@
     (part,) = call(
         functools.partial(transport_kernel, False), (FIELD,), "second_substep", energy, fields
     )
+    (part,) = call(near_kernel, (FIELD,), "near_flux", part, chip_in, *sides, fields)
     out = pl.pallas_call(
-        finish_kernel,
+        far_kernel,
         out_shape=shape(rows),
-        in_specs=[VMEM] * 7,
+        in_specs=[VMEM] * 4,
         out_specs=HBM,
         scratch_shapes=[
             pltpu.VMEM((PADF * 2 * ND, LANES), F32),
             pltpu.SemaphoreType.DMA((GROUPS,)),
         ],
         compiler_params=PARAMS,
-        name="finish",
-    )(part, cross, late_in, chip_in, *sides, fields)
+        name="far_flux",
+    )(part, cross, late_in, fields)
     return out.reshape(spectrum.shape)
 
 

time: 30.9 us -> 29.8 us (0.964)
  the two profiles are of different devices: /device:TPU:128 before, /device:TPU:4 now
where the time goes in v4:
time: 29.8 us; the launch traced here: 29.7 us
  waiting for transfers between devices  13.2 us (44%)
  Pallas kernels  12.6 us (42%)
  starting transfers between devices  3.87 us (13%)
    pallas_call x4, Pallas kernels, call(): pl.pallas_call(kernel, out_shape=[shape(rows) for rows in outs], in_specs...  7.56 us
    ppermute x4, waiting for transfers between devices, swap_columns(): lax.ppermute(side, ('geo', 'spec'), both(pairs))  7.3 us
    ppermute x2, waiting for transfers between devices, swap_cross(): return lax.ppermute(packet, ('geo', 'spec'), both(links))  5.93 us
    ppermute x4, starting transfers between devices, swap_columns(): lax.ppermute(side, ('geo', 'spec'), both(pairs))  3.58 us
    pallas_call x1, Pallas kernels, per_device(): pl.pallas_call(source_kernel, out_shape=[shape(n) for n in (FIELD, PACKET...  3.51 us
    pallas_call x1, Pallas kernels, per_device(): pl.pallas_call(far_kernel, out_shape=shape(rows), in_specs=[VMEM] * 4, ou...  1.49 us
  transfers between devices with their start and end apart: 8, of which 4 were waited for; matrix products, arithmetic and copies ran while one was open for 0% of the time, Pallas kernels for 25%

profile of v4, /device:TPU:4, one launch (start us, length us, event | category | flops | bytes accessed | tf_op | source)
XLA Modules:
  0.0 29.7 jit_solution(6022205401628876147)
XLA Ops:
  0.0 3.5 %source.1 = (f32[4032,128]{1,0:T(8,128)S(1)}, f32[1408,128]{1,0:T(8,128)S(1)}, f32[112,128]{1,0:T(8,128)S(1)}, f32[80,128]{1,0:T(8,128)S(1)}) custom-call(f32[3600,128]{1,0:T(8,128)} %bitcast.2, f32[2,128]{1,0:T(2,128)} %refs_1_.1, f32[2,128]{1,0:T(2,128)} %refs_2_.1, f32[2,512]{1,0:T(2,128)} %refs_3_.1, f32[2,512]{1,0:T(2,128)} %refs_4_.1, ...), custom_call_target="tpu_custom_call" | custom-call | tf_op jit(solution)/shard_map/source/pallas_call | solution.py:543
  3.5 1.3 %collective-permute-start.1 = (f32[112,128]{1,0:T(8,128)S(1)}, f32[112,128]{1,0:T(8,128)S(1)}, u32[]{:S(2)}, u32[]{:S(2)}) collective-permute-start(f32[112,128]{1,0:T(8,128)S(1)} %get-tuple-element.16), channel_id=1, source_target_pairs={{0,1},{2,3},{4,5},{6,7},{8,9},{10,11},{12,13},{14,15},{16,17},{18,... | collective-permute-start | bytes 172040 | tf_op jit(solution)/shard_map/ppermute | solution.py:533
  4.8 1.6 %collective-permute-start = (f32[112,128]{1,0:T(8,128)S(1)}, f32[112,128]{1,0:T(8,128)S(1)}, u32[]{:S(2)}, u32[]{:S(2)}) collective-permute-start(f32[112,128]{1,0:T(8,128)S(1)} %get-tuple-element.16), channel_id=1, source_target_pairs={{1,2},{5,6},{9,10},{13,14},{17,18},{21,22},{25,26},{29,30},{33,34}... | collective-permute-start | bytes 172040 | tf_op jit(solution)/shard_map/ppermute | solution.py:533
  6.4 0.0 collective-permute-start.2
  6.4 1.4 %collective-permute-done.1.refs_2_ = f32[112,128]{1,0:T(8,128)S(1)} collective-permute-done((f32[112,128]{1,0:T(8,128)S(1)}, f32[112,128]{1,0:T(8,128)S(1)}, u32[]{:S(2)}, u32[]{:S(2)}) %collective-permute-start.1) | collective-permute-done | bytes 57376 | tf_op jit(solution)/shard_map/ppermute | solution.py:533
  7.8 1.2 %collective-permute-done.refs_1_ = f32[112,128]{1,0:T(8,128)S(1)} collective-permute-done((f32[112,128]{1,0:T(8,128)S(1)}, f32[112,128]{1,0:T(8,128)S(1)}, u32[]{:S(2)}, u32[]{:S(2)}) %collective-permute-start) | collective-permute-done | bytes 57376 | tf_op jit(solution)/shard_map/ppermute | solution.py:533
  9.0 2.6 %first_substep.1 = (f32[4032,128]{1,0:T(8,128)S(1)}, f32[1416,128]{1,0:T(8,128)S(1)}, f32[1408,128]{1,0:T(8,128)S(1)}) custom-call(f32[4032,128]{1,0:T(8,128)S(1)} %get-tuple-element.15.refs_0_, f32[112,128]{1,0:T(8,128)S(1)} %collective-permute-done.refs_1_, f32[112,128]{1,0:T(8,128)S(1)} %collective-permute-done.1.refs_2_, ...), custom_call_target="tpu_custom_call" | custom-call | flops 20000000000 | tf_op jit(solution)/shard_map/first_substep/pallas_call | solution.py:499
  11.6 0.1 collective-permute-start.3
  11.7 0.1 collective-permute-start.7
  11.8 5.9 %collective-permute-done.2.cross_in = f32[1408,128]{1,0:T(8,128)S(1)} collective-permute-done((f32[1408,128]{1,0:T(8,128)S(1)}, f32[1408,128]{1,0:T(8,128)S(1)}, u32[]{:S(2)}, u32[]{:S(2)}) %collective-permute-start.2) | collective-permute-done | bytes 720928 | tf_op jit(solution)/shard_map/ppermute | solution.py:519
  17.7 0.0 collective-permute-done.3.chip_in
  17.7 1.2 %complete.1 = (f32[4032,128]{1,0:T(8,128)S(1)}, f32[1408,128]{1,0:T(8,128)S(1)}, f32[112,128]{1,0:T(8,128)S(1)}) custom-call(f32[4032,128]{1,0:T(8,128)S(1)} %get-tuple-element.18.part_ref, f32[1408,128]{1,0:T(8,128)S(1)} %collective-permute-done.2.cross_in, f32[1408,128]{1,0:T(8,128)S(1)} %collective-permute-done.3.chip_in, ...), custom_call_target="tpu_custom_call" | custom-call | tf_op jit(solution)/shard_map/complete/pallas_call | solution.py:499
  18.9 0.1 collective-permute-start.4
  19.0 0.1 collective-permute-start.6
  19.1 0.6 %collective-permute-start.5 = (f32[112,128]{1,0:T(8,128)S(1)}, f32[112,128]{1,0:T(8,128)S(1)}, u32[]{:S(2)}, u32[]{:S(2)}) collective-permute-start(f32[112,128]{1,0:T(8,128)S(1)} %get-tuple-element.23), channel_id=1, source_target_pairs={{1,2},{5,6},{9,10},{13,14},{17,18},{21,22},{25,26},{29,30},{33,34}... | collective-permute-start | bytes 172040 | tf_op jit(solution)/shard_map/ppermute | solution.py:533
  19.7 2.2 %second_substep.1.part_ref = f32[4032,128]{1,0:T(8,128)S(1)} custom-call(f32[4032,128]{1,0:T(8,128)S(1)} %get-tuple-element.21.refs_0_, f32[80,128]{1,0:T(8,128)S(1)} %get-tuple-element.17.refs_3_.fields_ref.refs_1_), custom_call_target="tpu_custom_call" | custom-call | tf_op jit(solution)/shard_map/second_substep/pallas_call | solution.py:499
  22.0 4.7 %collective-permute-done.6.side_b = f32[112,128]{1,0:T(8,128)S(1)} collective-permute-done((f32[112,128]{1,0:T(8,128)S(1)}, f32[112,128]{1,0:T(8,128)S(1)}, u32[]{:S(2)}, u32[]{:S(2)}) %collective-permute-start.6) | collective-permute-done | bytes 57376 | tf_op jit(solution)/shard_map/ppermute | solution.py:533
  26.7 0.0 collective-permute-done.5.side_a
  26.7 0.0 collective-permute-done.4.chip_in
  26.7 1.5 %near_flux.1.part_ref = f32[4032,128]{1,0:T(8,128)S(1)} custom-call(f32[4032,128]{1,0:T(8,128)S(1)} %second_substep.1.part_ref, f32[1408,128]{1,0:T(8,128)S(1)} %collective-permute-done.4.chip_in, f32[112,128]{1,0:T(8,128)S(1)} %collective-permute-done.5.side_a, f32[112,128]{1,0:T(8,128)S(1)} %collective-permute-done.6.side_b, ...), custom_call_target="tpu_custom_call" | custom-call | tf_op jit(solution)/shard_map/near_flux/pallas_call | solution.py:499
  28.2 0.0 collective-permute-done.7.cross_in
  28.2 1.5 %far_flux.1 = f32[3600,128]{1,0:T(8,128)} custom-call(f32[4032,128]{1,0:T(8,128)S(1)} %near_flux.1.part_ref, f32[1408,128]{1,0:T(8,128)S(1)} %get-tuple-element.19.sent_ref, f32[1416,128]{1,0:T(8,128)S(1)} %collective-permute-done.7.cross_in, f32[80,128]{1,0:T(8,128)S(1)} %get-tuple-element.17.refs_3_.fields_ref.refs_1_), custom_call_target="tpu_custom_call" | custom-call | tf_op jit(solution)/shard_map/far_flux/pallas_call | solution.py:576
Async XLA Ops:
  3.5 4.3 %collective-permute-start.1 = (f32[112,128]{1,0:T(8,128)S(1)}, f32[112,128]{1,0:T(8,128)S(1)}, u32[]{:S(2)}, u32[]{:S(2)}) collective-permute-start(f32[112,128]{1,0:T(8,128)S(1)} %get-tuple-element.16), channel_id=1, source_target_pairs={{0,1},{2,3},{4,5},{6,7},{8,9},{10,11},{12,13},{14,15},{16,17},{18,... | collective-permute-start | bytes 172040 | tf_op jit(solution)/shard_map/ppermute | solution.py:533
  4.8 4.2 %collective-permute-start = (f32[112,128]{1,0:T(8,128)S(1)}, f32[112,128]{1,0:T(8,128)S(1)}, u32[]{:S(2)}, u32[]{:S(2)}) collective-permute-start(f32[112,128]{1,0:T(8,128)S(1)} %get-tuple-element.16), channel_id=1, source_target_pairs={{1,2},{5,6},{9,10},{13,14},{17,18},{21,22},{25,26},{29,30},{33,34}... | collective-permute-start | bytes 172040 | tf_op jit(solution)/shard_map/ppermute | solution.py:533
  6.4 11.3 %collective-permute-start.2 = (f32[1408,128]{1,0:T(8,128)S(1)}, f32[1408,128]{1,0:T(8,128)S(1)}, u32[]{:S(2)}, u32[]{:S(2)}) collective-permute-start(f32[1408,128]{1,0:T(8,128)S(1)} %get-tuple-element.19.sent_ref), channel_id=1, source_target_pairs={{4,8},{5,9},{6,10},{7,11},{12,16},{13,17},{14,18},{15,19},{20,24},... | collective-permute-start | bytes 2162696 | tf_op jit(solution)/shard_map/ppermute | solution.py:519
  11.6 6.1 %collective-permute-start.3 = (f32[1408,128]{1,0:T(8,128)S(1)}, f32[1408,128]{1,0:T(8,128)S(1)}, u32[]{:S(2)}, u32[]{:S(2)}) collective-permute-start(f32[1408,128]{1,0:T(8,128)S(1)} %get-tuple-element.20), channel_id=1, source_target_pairs={{0,4},{8,12},{16,20},{24,28},{32,36},{40,44},{48,52},{56,60},{64,6... | collective-permute-start | bytes 2162696 | tf_op jit(solution)/shard_map/ppermute | solution.py:524
  11.7 16.6 %collective-permute-start.7 = (f32[1416,128]{1,0:T(8,128)S(1)}, f32[1416,128]{1,0:T(8,128)S(1)}, u32[]{:S(2)}, u32[]{:S(2)}) collective-permute-start(f32[1416,128]{1,0:T(8,128)S(1)} %get-tuple-element.24), channel_id=1, source_target_pairs={{4,8},{5,9},{6,10},{7,11},{12,16},{13,17},{14,18},{15,19},{20,24},... | collective-permute-start | bytes 2174984 | tf_op jit(solution)/shard_map/ppermute | solution.py:519
  18.9 7.8 %collective-permute-start.4 = (f32[1408,128]{1,0:T(8,128)S(1)}, f32[1408,128]{1,0:T(8,128)S(1)}, u32[]{:S(2)}, u32[]{:S(2)}) collective-permute-start(f32[1408,128]{1,0:T(8,128)S(1)} %get-tuple-element.22), channel_id=1, source_target_pairs={{0,4},{8,12},{16,20},{24,28},{32,36},{40,44},{48,52},{56,60},{64,6... | collective-permute-start | bytes 2162696 | tf_op jit(solution)/shard_map/ppermute | solution.py:524
  19.0 7.7 %collective-permute-start.6 = (f32[112,128]{1,0:T(8,128)S(1)}, f32[112,128]{1,0:T(8,128)S(1)}, u32[]{:S(2)}, u32[]{:S(2)}) collective-permute-start(f32[112,128]{1,0:T(8,128)S(1)} %get-tuple-element.23), channel_id=1, source_target_pairs={{0,1},{2,3},{4,5},{6,7},{8,9},{10,11},{12,13},{14,15},{16,17},{18,... | collective-permute-start | bytes 172040 | tf_op jit(solution)/shard_map/ppermute | solution.py:533
  19.1 7.6 %collective-permute-start.5 = (f32[112,128]{1,0:T(8,128)S(1)}, f32[112,128]{1,0:T(8,128)S(1)}, u32[]{:S(2)}, u32[]{:S(2)}) collective-permute-start(f32[112,128]{1,0:T(8,128)S(1)} %get-tuple-element.23), channel_id=1, source_target_pairs={{1,2},{5,6},{9,10},{13,14},{17,18},{21,22},{25,26},{29,30},{33,34}... | collective-permute-start | bytes 172040 | tf_op jit(solution)/shard_map/ppermute | solution.py:533
